TPU v7x, 256 devices: a whole 4x4x8 slice. The times are simulated.
256 devices in a mesh: site: 4 (over y), blk: 64 (over z, x, core).
Axes of the slice: x: 4, y: 4, z: 8, core: 2. Of those that a mesh axis runs over, the one named last changes fastest.
Arguments:
- sgt: bfloat16 [4, 2, 6, 2, 8192, 1024], P('site', None, None, None, 'blk'), may hold values from -6 to 6
- mechanism: float32 [6, 8192], P(None, 'blk'), may hold values from -2.5 to 2.5
- slip_fields: float32 [256, 3, 8192], P('blk', None, 'site'), may hold values from 0 to 20, as said below
- rupture_start: int32 [256], replicated, may hold values from 0 to 63, as said below
- point_count: int32 [256], replicated, may hold values from 32 to 2048, as said below
- owner_order: int32 [256], replicated, may hold values from 0 to 255, as said below
Outputs:
- spectral_accel: float32 [4, 256, 88], P('site', 'blk')
Inputs may be any that keep to these rules, and one draw needn't show every extreme that they name: `point_count`: each variation's points lie within the fault. rupture_start[v] + ceil(point_count[v] / 128) <= 64. `owner_order`: a permutation; the variations held in the 4 slots j of one owner (equal j // 4) touch disjoint sets of fault blocks. `slip_fields`: channel 0 (slip) lies in 0.2 to 2, channel 1 (onset) in 0 to 20, channel 2 (rise time) in 0.05 to 0.5.
All inputs are finite; a program needn't handle non-finite values.
Results may differ from a plain program's by a relative error of at most 0.00084.
Values sent between devices are 32-bit elements; how exact they have to be, the bound alone decides.
A program may use at most 128 MiB of HBM per device.

v0:
```python
import jax
import jax.numpy as jnp
from jax import lax
from jax.sharding import PartitionSpec as P

PERIODS = 44


DT = 0.1
DAMPING = 0.05
group_rows = 8


def angular(freq_count):
    return 2.0 * jnp.pi * jnp.arange(freq_count, dtype=jnp.float32) / (2 * freq_count * DT)


def source_terms(slip_amp, onset, rise_time, active, omega):
    scaled = jnp.where(active, slip_amp, 0.0)[..., None] / jnp.sqrt(
        1.0 + (omega * rise_time[..., None]) ** 2
    )
    phase = omega * onset[..., None]
    return (scaled * jnp.cos(phase), scaled * jnp.sin(phase))


def contract(cosine_part, sine_part, w_real, w_imag):
    w_real = w_real.astype(jnp.float32)
    w_imag = w_imag.astype(jnp.float32)
    real_sum = jnp.sum(cosine_part * w_real + sine_part * w_imag, axis=-2)
    imag_sum = jnp.sum(cosine_part * w_imag - sine_part * w_real, axis=-2)
    return jnp.stack([real_sum, imag_sum], axis=-2)


def dft_tables(freq_count):
    samples = 2 * freq_count
    freq_ids = jnp.arange(freq_count, dtype=jnp.int32)
    time_ids = jnp.arange(samples, dtype=jnp.int32)
    product = freq_ids[:, None] * time_ids[None, :] % samples
    angle = 2.0 * jnp.pi * product.astype(jnp.float32) / samples
    factor = jnp.where(freq_ids == 0, 1.0, 2.0).astype(jnp.float32) / freq_count
    return (factor[:, None] * jnp.cos(angle), factor[:, None] * jnp.sin(angle))


def oscillator_peaks(spectra, omega):
    freq_count = spectra.shape[-1]
    steps = jnp.arange(PERIODS, dtype=jnp.float32) / (PERIODS - 1)
    natural = 2.0 * jnp.pi / (0.2 * 50.0**steps)
    stiffness = natural[:, None] ** 2 - omega[None, :] ** 2
    friction = 2.0 * DAMPING * natural[:, None] * omega[None, :]
    gain_factor = natural[:, None] ** 2 / (stiffness**2 + friction**2)
    real_part = spectra[:, :, 0, None, :]
    imag_part = spectra[:, :, 1, None, :]
    resp_real = gain_factor * (real_part * stiffness + imag_part * friction)
    resp_imag = gain_factor * (imag_part * stiffness - real_part * friction)
    cosine, sine = dft_tables(freq_count)
    series = jnp.dot(
        resp_real.reshape(-1, freq_count),
        cosine,
        precision=lax.Precision.HIGHEST,
        preferred_element_type=jnp.float32,
    )
    series = series - jnp.dot(
        resp_imag.reshape(-1, freq_count),
        sine,
        precision=lax.Precision.HIGHEST,
        preferred_element_type=jnp.float32,
    )
    return jnp.max(jnp.abs(series), axis=1).reshape(spectra.shape[0], 2 * PERIODS)


def per_device(sgt, mechanism, slip_fields, rupture_start, point_count, owner_order):
    block_pts = sgt.shape[4]
    freq_count = sgt.shape[5]
    blk_count = lax.axis_size("blk")
    var_dev = slip_fields.shape[0]
    total_vars = var_dev * blk_count
    total = jnp.zeros((2, 2, block_pts, freq_count), jnp.float32)
    for component in range(6):
        total = total + mechanism[component][None, None, :, None] * sgt[0, :, component].astype(
            jnp.float32
        )
    weights = total.astype(jnp.bfloat16)
    whole_fault = lax.all_gather(slip_fields, "site", axis=2, tiled=True)
    local_slip = lax.all_to_all(whole_fault, "blk", split_axis=2, concat_axis=0, tiled=True)
    own_block = lax.axis_index("blk")
    variation_ids = jnp.arange(total_vars, dtype=jnp.int32)
    block_span = (point_count + block_pts - 1) // block_pts
    touching = (rupture_start <= own_block) & (own_block < rupture_start + block_span)
    offset = (own_block - rupture_start) * block_pts
    slot_of = jnp.sum(
        jnp.where(owner_order[None, :] == variation_ids[:, None], variation_ids[None, :], 0), axis=1
    )
    omega = angular(freq_count)
    point_ids = jnp.arange(block_pts, dtype=jnp.int32)
    sort_keys = jnp.where(touching, 0, 1) * total_vars + variation_ids
    ranking = jnp.argsort(sort_keys, stable=True)
    ranking = jnp.concatenate([ranking, jnp.zeros((group_rows,), jnp.int32)])
    live_count = jnp.sum(touching.astype(jnp.int32))
    turns = (live_count + group_rows - 1) // group_rows

    def one_turn(turn_index, buffer):
        position = turn_index * group_rows + jnp.arange(group_rows, dtype=jnp.int32)
        picked = lax.dynamic_slice_in_dim(ranking, turn_index * group_rows, group_rows)
        is_live = position < live_count
        fields = local_slip[picked]
        point_index = offset[picked][:, None] + point_ids[None, :]
        active = is_live[:, None] & (point_index < point_count[picked][:, None])
        cosine_part, sine_part = source_terms(
            fields[:, 0], fields[:, 1], fields[:, 2], active, omega
        )
        spectrum = contract(cosine_part[:, None], sine_part[:, None], weights[:, 0], weights[:, 1])
        return buffer.at[slot_of[picked]].add(spectrum)

    owned_rows = lax.psum_scatter(
        lax.fori_loop(0, turns, one_turn, jnp.zeros((total_vars, 2, 2, freq_count), jnp.float32)),
        "blk",
        scatter_dimension=0,
        tiled=True,
    )
    return oscillator_peaks(owned_rows, omega)[None]


def solution(mesh):
    return jax.shard_map(
        per_device,
        mesh=mesh,
        in_specs=(
            P("site", None, None, None, "blk", None),
            P(None, "blk"),
            P("blk", None, "site"),
            P(),
            P(),
            P(),
        ),
        out_specs=P("site", "blk", None),
        check_vma=False,
    )
```

profile of v0, /device:TPU:1, one launch (start us, length us, event | category | flops | bytes accessed | tf_op | source)
XLA Modules:
  0.0 459.1 jit_solution(13625285809886444630)
XLA Ops:
  6.5 12.2 %all_gather.3 = f32[4,3,8192]{2,0,1:T(4,128)S(1)} all-gather(f32[4,3,2048]{2,0,1:T(4,128)} %param.10), channel_id=1, replica_groups=mesh['site'=4,'blk'=64] {'site'}, dimensions={2}, use_global_device_ids=true | all-gather | bytes 491520 | tf_op jit(solution)/shard_map/all_gather | solution.py:83
  18.8 10.7 %copy.46 = f32[4,3,8192]{0,1,2:T(4,128)} copy(f32[4,3,8192]{2,0,1:T(4,128)S(1)} %all_gather.3) | data formatting | bytes 786432 | tf_op jit(solution)/shard_map/all_gather | solution.py:83
  29.5 16.7 %reshape.362 = f32[64,1,1536]{2,1,0:T(1,128)} reshape(f32[8192,3,4]{2,1,0:T(4,128)} %bitcast.90) | data formatting | bytes 786432
  46.2 14.0 %all-to-all-start = ((f32[64,1,1536]{2,1,0:T(1,128)}), f32[64,1,1536]{2,1,0:T(1,128)S(1)}, u32[]{:S(2)}, u32[]{:S(2)}) async-start(f32[64,1,1536]{2,1,0:T(1,128)} %reshape.362), calls=%async_computation | async-start | bytes 786432 | tf_op jit(solution)/shard_map/all_to_all | solution.py:84
  61.7 5.2 %fusion.45 = (bf16[1,2,1,2,128,1024]{5,4,3,2,1,0:T(8,128)(2,1)S(1)}, bf16[1,2,1,2,128,1024]{5,4,3,2,1,0:T(8,128)(2,1)S(1)}, bf16[1,2,1,2,128,1024]{5,4,3,2,1,0:T...) fusion(bf16[1,2,6,2,128,1024]{5,4,3,2,1,0:T(8,128)(2,1)} %param.8), kind=kLoop, calls=%fused_computation.104 | loop fusion | bytes 12582912 | tf_op jit(solution)/shard_map/slice | solution.py:79
  66.9 3.2 sort.17
  72.4 3.9 fusion.29
  78.4 11.6 %reshape.363 = f32[8192,3,4]{2,1,0:T(4,128)} reshape(f32[64,1536]{1,0:T(8,128)S(1)} %reduce) | data formatting | bytes 786432
  90.0 12.4 %copy.47 = f32[64,4,3,128]{3,2,1,0:T(4,128)S(1)} copy(f32[64,4,3,128]{1,2,3,0:T(4,128)} %bitcast.91) | data formatting | bytes 786432 | tf_op jit(solution)/shard_map/all_to_all | solution.py:84
  102.4 4.1 broadcast_in_dim.30
  106.5 73.0 %while.12 = (s32[]{:T(128)}, f32[256,2,2,1024]{3,2,1,0:T(2,128)}, s32[]{:T(128)}, s32[264]{0:T(512)S(1)}, s32[256]{0:T(256)S(1)}, /*index=5*/s32[]{:T(128)}, s32...) while((s32[]{:T(128)}, f32[256,2,2,1024]{3,2,1,0:T(2,128)}, ...), condition=%wide.region_7.8_spmd.clone.clone, body=%wide.region_3.7_spmd.clone.clone.sunk | while | flops 24680516 | bytes 23151376 | solution.py:115
  109.2 15.7 %fusion.65 = (f32[8,128,1024]{2,1,0:T(8,128)S(1)}, f32[8,128,1024]{2,1,0:T(8,128)S(1)}) fusion(f32[8,128]{1,0:T(8,128)S(1)} %bitcast.96, f32[8,128]{1,0:T(8,128)S(1)} %bitcast.95, f32[1024]{0:T(1024)S(1)} %iota_multiply_fusion.3, f32[8,128]{1,0:T(8,128)S(1)} %fusion.64), kind=kLoop, calls=%fused_computation.11.clone.1 | loop fusion | flops 7340032 | bytes 8404992 | tf_op jit(solution)/shard_map/while/body/mul | solution.py:23
  125.2 2.5 add_reduce_fusion.2
  133.5 15.7 %fusion.65 = (f32[8,128,1024]{2,1,0:T(8,128)S(1)}, f32[8,128,1024]{2,1,0:T(8,128)S(1)}) fusion(f32[8,128]{1,0:T(8,128)S(1)} %bitcast.96, f32[8,128]{1,0:T(8,128)S(1)} %bitcast.95, f32[1024]{0:T(1024)S(1)} %iota_multiply_fusion.3, f32[8,128]{1,0:T(8,128)S(1)} %fusion.64), kind=kLoop, calls=%fused_computation.11.clone.1 | loop fusion | flops 7340032 | bytes 8404992 | tf_op jit(solution)/shard_map/while/body/mul | solution.py:23
  149.5 2.5 add_reduce_fusion.2
  152.8 2.4 scatter_fusion
  157.9 15.7 %fusion.65 = (f32[8,128,1024]{2,1,0:T(8,128)S(1)}, f32[8,128,1024]{2,1,0:T(8,128)S(1)}) fusion(f32[8,128]{1,0:T(8,128)S(1)} %bitcast.96, f32[8,128]{1,0:T(8,128)S(1)} %bitcast.95, f32[1024]{0:T(1024)S(1)} %iota_multiply_fusion.3, f32[8,128]{1,0:T(8,128)S(1)} %fusion.64), kind=kLoop, calls=%fused_computation.11.clone.1 | loop fusion | flops 7340032 | bytes 8404992 | tf_op jit(solution)/shard_map/while/body/mul | solution.py:23
  173.8 2.5 add_reduce_fusion.2
  177.2 2.4 scatter_fusion
  179.5 32.0 %fusion.54 = f32[1024,2048]{1,0:T(8,128)} fusion(f32[1024]{0:T(1024)S(1)} %select_multiply_fusion), kind=kLoop, calls=%fused_computation.34.clone.1 | loop fusion | flops 31457280 | bytes 8392704 | tf_op jit(solution)/shard_map/dot_general | solution.py:62
  211.5 31.7 %fusion.56 = f32[1024,2048]{1,0:T(8,128)} fusion(f32[1024]{0:T(1024)S(1)} %select_multiply_fusion), kind=kLoop, calls=%fused_computation.37.clone.clone.clone.1 | loop fusion | flops 31457280 | bytes 8392704 | tf_op jit(solution)/shard_map/dot_general | solution.py:56
  243.3 178.3 %all-reduce.4.cloned.1.call-done = f32[256,2,2,1024]{3,2,1,0:T(2,128)} async-done(((f32[256,2,2,1024]{3,2,1,0:T(2,128)}), f32[256,2,2,1024]{3,2,1,0:T(2,128)}) %all-reduce.4.cloned.1.call-update) | async-done | bytes 4194320
  426.9 12.1 %fusion.13 = f32[352,2048]{1,0:T(8,128)S(1)} fusion(f32[352,1024]{1,0:T(8,128)S(1)} %mul.423, f32[1024,2048]{1,0:T(8,128)} %fusion.54), kind=kOutput, calls=%fused_computation.33 | convolution fusion | flops 8858370048 | bytes 12713984 | tf_op jit(solution)/shard_map/dot_general | solution.py:62
  439.0 12.5 %abs_reduce_fusion = f32[352]{0:T(512)S(1)} fusion(f32[352,2048]{1,0:T(8,128)S(1)} %fusion.13, f32[352,1024]{1,0:T(8,128)S(1)} %copy-done.1, f32[1024,2048]{1,0:T(8,128)} %fusion.56), kind=kOutput, calls=%fused_computation.44 | convolution fusion | flops 8860532736 | bytes 12715392 | tf_op jit(solution)/shard_map/dot_general | solution.py:56
  (83 shorter events, 24.1 us)
Async XLA Ops:
  29.5 30.8 %copy-start = (s32[256]{0:T(256)S(1)}, s32[256]{0:T(256)}, u32[]{:S(2)}) copy-start(s32[256]{0:T(256)} %param.12) | copy-start | bytes 3076
  29.5 30.8 %copy-start.6 = (s32[256]{0:T(256)S(1)}, s32[256]{0:T(256)}, u32[]{:S(2)}) copy-start(s32[256]{0:T(256)} %param.11) | copy-start | bytes 3076
  46.2 30.1 %all-to-all-start = ((f32[64,1,1536]{2,1,0:T(1,128)}), f32[64,1,1536]{2,1,0:T(1,128)S(1)}, u32[]{:S(2)}, u32[]{:S(2)}) async-start(f32[64,1,1536]{2,1,0:T(1,128)} %reshape.362), calls=%async_computation | async-start | bytes 786432 | tf_op jit(solution)/shard_map/all_to_all | solution.py:84
  60.2 361.3 %all-reduce.4.cloned.1.call-start = ((), (), s32[]{:S(2)}) async-start(), calls=%async_computation.1 | async-start | bytes 8388608
  61.6 8.4 %copy-start.7 = (s32[256]{0:T(256)S(1)}, s32[256]{0:T(256)}, u32[]{:S(2)}) copy-start(s32[256]{0:T(256)} %param.13) | copy-start | bytes 3076
  61.7 8.5 %copy-start.8 = (u32[256]{0:T(256)S(1)}, u32[256]{0:T(256)}, u32[]{:S(2)}) copy-start(u32[256]{0:T(256)} %constant.112) | copy-start | bytes 3076
  61.7 10.7 %copy-start.5 = (f32[6,128]{1,0:T(8,128)S(1)}, f32[6,128]{1,0:T(8,128)}, u32[]{:S(2)}) copy-start(f32[6,128]{1,0:T(8,128)} %param.9) | copy-start | bytes 9220
  211.5 211.0 %copy-start.2 = (f32[44,1024]{1,0:T(8,128)S(1)}, f32[44,1024]{1,0:T(8,128)}, u32[]{:S(2)}) copy-start(f32[44,1024]{1,0:T(8,128)} %get-tuple-element.168) | copy-start | bytes 540676
  211.5 211.0 %copy-start.3 = (f32[44,1024]{1,0:T(8,128)S(1)}, f32[44,1024]{1,0:T(8,128)}, u32[]{:S(2)}) copy-start(f32[44,1024]{1,0:T(8,128)} %get-tuple-element.169) | copy-start | bytes 540676
  211.5 211.0 %copy-start.4 = (f32[44,1024]{1,0:T(8,128)S(1)}, f32[44,1024]{1,0:T(8,128)}, u32[]{:S(2)}) copy-start(f32[44,1024]{1,0:T(8,128)} %get-tuple-element.170) | copy-start | bytes 540676
  426.9 12.1 %copy-start.1 = (f32[352,1024]{1,0:T(8,128)S(1)}, f32[352,1024]{1,0:T(8,128)}, u32[]{:S(2)}) copy-start(f32[352,1024]{1,0:T(8,128)} %mul.414) | copy-start | bytes 4325380
Sparse Core Ops, SparseCore 0:
  179.7 241.8 all-reduce.3
where the time goes:
time: 461 us; the launch traced here: 459 us
  waiting for transfers between devices  178 us (39%)
  other arithmetic  141 us (31%)
  local copies, waits for them, and re-layouts  74.2 us (16%)
  matrix products  24.6 us (5%)
  between operations  14.9 us (3%)
  starting transfers between devices  14 us (3%)
  blocking collectives  12.2 us (3%)
    unnamed x2, waiting for transfers between devices  178 us
    mul x3, other arithmetic, source_terms(): return (scaled * jnp.cos(phase), scaled * jnp.sin(phase))  47.1 us
    dot_general x1, other arithmetic, oscillator_peaks(): jnp.dot(resp_imag.reshape(-1, freq_count), sine, precision=lax.Precision....  32 us
    dot_general x1, other arithmetic, oscillator_peaks(): jnp.dot(resp_real.reshape(-1, freq_count), cosine, precision=lax.Precisio...  31.7 us
    unnamed x22, local copies, waits for them, and re-layouts  29 us
    all_to_all x1, starting transfers between devices, per_device(): lax.all_to_all(whole_fault, 'blk', split_axis=2, concat_axis=0, tiled=True)  14 us
    all_to_all x2, local copies, waits for them, and re-layouts, per_device(): lax.all_to_all(whole_fault, 'blk', split_axis=2, concat_axis=0, tiled=True)  12.9 us
    dot_general x1, matrix products, oscillator_peaks(): jnp.dot(resp_real.reshape(-1, freq_count), cosine, precision=lax.Precisio...  12.5 us
  transfers between devices with their start and end apart: 2, of which 1 were waited for; matrix products, arithmetic and copies ran while one was open for 17% of the time, Pallas kernels for 0%

commit v1 on v0

v1 whole, which is shorter than its diff:
```python
import functools

import jax
import jax.numpy as jnp
import ml_dtypes
import numpy as np
from jax import lax
from jax.experimental import pallas as pl
from jax.experimental.pallas import tpu as pltpu
from jax.sharding import PartitionSpec as P

MESH = pl.DeviceIdType.MESH
FREQ = 1024
PERIODS = 44
PAD_PERIODS = 48
PTS = 128
SITES = 4
NZ = 8
NJ = 8
OWNERS = NZ * NJ
CHUNKS = 4
STEPS = 16
ROWS = 8 * PAD_PERIODS
HALF = FREQ // 2
DT = 0.1
DAMPING = 0.05
TURNS = 1.0 / (2 * FREQ * DT)
F32 = jnp.float32
BF16 = jnp.bfloat16


def split_table(table):
    high = table.astype(ml_dtypes.bfloat16)
    low = (table - high.astype(np.float64)).astype(ml_dtypes.bfloat16)
    return high, low


def constant_tables():
    freq = np.arange(FREQ)
    omega = 2 * np.pi * freq * TURNS
    factor = np.where(freq == 0, 1.0, 2.0) / FREQ
    natural = 2 * np.pi / (0.2 * 50.0 ** (np.arange(PERIODS) / (PERIODS - 1)))
    stiffness = natural[:, None] ** 2 - omega[None] ** 2
    friction = 2 * DAMPING * natural[:, None] * omega[None]
    gain = factor[None] * natural[:, None] ** 2 / (stiffness**2 + friction**2)
    response = np.zeros((2, 2, PAD_PERIODS, HALF), np.float32)
    for parity in range(2):
        response[parity, 0, :PERIODS] = (gain * stiffness)[:, parity::2]
        response[parity, 1, :PERIODS] = (gain * friction)[:, parity::2]
    sample = np.arange(HALF)
    tables = np.zeros((2, 2, 2, HALF, HALF), ml_dtypes.bfloat16)
    for parity in range(2):
        ids = freq[parity::2]
        angle = 2 * np.pi * ((ids[:, None] * sample[None]) % (2 * FREQ)) / (2 * FREQ)
        tables[parity, 0, 0], tables[parity, 0, 1] = split_table(np.cos(angle))
        sine = np.sin(angle)
        if parity == 1:
            sine[:, 0] = np.where(np.arange(HALF) % 2 == 0, 1.0, -1.0)
        tables[parity, 1, 0], tables[parity, 1, 1] = split_table(sine)
    return response, tables


def place():
    y = lax.axis_index("site")
    b = lax.axis_index("blk")
    return y, b, lax.div(b, NJ), lax.rem(b, NJ)


def greet(peers):
    barrier = pltpu.get_barrier_semaphore()
    for peer in peers:
        pl.semaphore_signal(barrier, inc=1, device_id=peer, device_id_type=MESH)
    pl.semaphore_wait(barrier, len(peers))


def remote(src, dst, send, recv, peer):
    return pltpu.make_async_remote_copy(
        src_ref=src, dst_ref=dst, send_sem=send, recv_sem=recv, device_id=peer, device_id_type=MESH
    )


def slip_kernel(
    start_ref, count_ref, order_ref, slip_ref, out_ref, mine, fault, plane, block,
    send_a, recv_a, send_b, recv_b, send_c, recv_c, send_d, recv_d,
):
    y, b, z, j = place()
    y_peers = [(lax.rem(y + d, SITES), b) for d in range(1, SITES)]
    j_peers = [(y, z * NJ + lax.rem(j + d, NJ)) for d in range(1, NJ)]
    z_peers = [(y, lax.rem(z + d, NZ) * NJ + j) for d in range(1, NZ)]
    greet(y_peers + j_peers + z_peers)
    for v in range(4):
        for zz in range(2):
            for jj in range(NJ):
                at = (zz * NJ + jj) * PTS
                mine[v, zz, jj, 0:3, :] = slip_ref[v, :, at : at + PTS]
    copies = []
    for d, peer in enumerate(y_peers):
        copy = remote(mine.at[peer[0]], fault.at[pl.ds(2 * y, 2)], send_a.at[d], recv_a.at[d], peer)
        copy.start()
        copies.append(copy)
    fault[pl.ds(2 * y, 2)] = mine[y]
    for copy in copies:
        copy.wait()
    copies = []
    for d, peer in enumerate(j_peers):
        target = lax.rem(j + d + 1, NJ)
        copy = remote(fault.at[:, target], plane.at[j], send_b.at[d], recv_b.at[d], peer)
        copy.start()
        copies.append(copy)
    plane[j] = fault[:, j]
    for copy in copies:
        copy.wait()
    copies = []
    for d, peer in enumerate(z_peers):
        target = lax.rem(z + d + 1, NZ)
        copy = remote(plane.at[:, target], block.at[y, z], send_c.at[d], recv_c.at[d], peer)
        copy.start()
        copies.append(copy)
    block[y, z] = plane[:, z]
    for copy in copies:
        copy.wait()
    copies = []
    for d, peer in enumerate(y_peers):
        copy = remote(block.at[y], block.at[y], send_d.at[d], recv_d.at[d], peer)
        copy.start()
        copies.append(copy)
    for copy in copies:
        copy.wait()

    lane = lax.broadcasted_iota(jnp.int32, (1, PTS), 1)

    def select(row, carry):
        owner = lax.rem(row, NZ) * NJ + lax.div(row, NZ)
        chosen = jnp.int32(0)
        points = jnp.int32(0)
        for slot in range(4):
            v = order_ref[owner * 4 + slot]
            first = start_ref[v]
            count = count_ref[v]
            left = count - (b - first) * PTS
            live = (first <= b) & (left > 0)
            chosen = jnp.where(live, v, chosen)
            points = jnp.where(live, left, points)
        fields = block[chosen & 3, lax.shift_right_logical(chosen, 5), lax.shift_right_logical(chosen, 2) & 7]
        out_ref[0, pl.ds(row, 1), :] = jnp.where(lane < points, fields[0:1], 0.0)
        out_ref[1, pl.ds(row, 1), :] = fields[1:2]
        out_ref[2, pl.ds(row, 1), :] = fields[2:3]
        return carry

    lax.fori_loop(0, OWNERS, select, 0)


def exchange_slip(slip, start, count, order):
    dma = pltpu.SemaphoreType.DMA
    smem = pl.BlockSpec(memory_space=pltpu.SMEM)
    vmem = pl.BlockSpec(memory_space=pltpu.VMEM)
    return pl.pallas_call(
        slip_kernel,
        out_shape=jax.ShapeDtypeStruct((3, OWNERS, PTS), F32),
        in_specs=[smem, smem, smem, vmem],
        out_specs=vmem,
        scratch_shapes=[
            pltpu.VMEM((4, 2, NJ, 4, PTS), F32),
            pltpu.VMEM((NZ, NJ, 4, PTS), F32),
            pltpu.VMEM((NJ, NZ, 4, PTS), F32),
            pltpu.VMEM((4, NZ, NJ, 4, PTS), F32),
            dma((3,)), dma((3,)), dma((7,)), dma((7,)), dma((7,)), dma((7,)), dma((3,)), dma((3,)),
        ],
        compiler_params=pltpu.CompilerParams(collective_id=0, has_side_effects=True),
        name="slip_exchange",
    )(start, count, order, slip)


def weights_kernel(sgt_ref, mech_ref, out_ref, mech_wide):
    turned = jnp.transpose(jnp.concatenate([mech_ref[...], jnp.zeros((2, PTS), F32)], axis=0))
    for k in range(6):
        mech_wide[k] = jnp.broadcast_to(turned[:, k : k + 1], (PTS, PTS))

    def tile(step, carry):
        at = pl.multiple_of(step * PTS, PTS)
        for c in range(2):
            for part in range(2):
                total = mech_wide[0] * sgt_ref[0, c, 0, part, :, pl.ds(at, PTS)].astype(F32)
                for k in range(1, 6):
                    total = total + mech_wide[k] * sgt_ref[0, c, k, part, :, pl.ds(at, PTS)].astype(F32)
                turned = jnp.transpose(total)
                rows = at * 4 + 2 * c
                if part == 0:
                    out_ref[0, pl.ds(rows, PTS, stride=4), :] = turned
                    out_ref[1, pl.ds(rows + 1, PTS, stride=4), :] = -turned
                else:
                    out_ref[1, pl.ds(rows, PTS, stride=4), :] = turned
                    out_ref[0, pl.ds(rows + 1, PTS, stride=4), :] = turned
        return carry

    lax.fori_loop(0, FREQ // PTS, tile, 0)


def make_weights(sgt, mechanism):
    vmem = pl.BlockSpec(memory_space=pltpu.VMEM)
    return pl.pallas_call(
        weights_kernel,
        out_shape=jax.ShapeDtypeStruct((2, FREQ * 4, PTS), F32),
        in_specs=[vmem, vmem],
        out_specs=vmem,
        scratch_shapes=[pltpu.VMEM((6, PTS, PTS), F32)],
        compiler_params=pltpu.CompilerParams(vmem_limit_bytes=32 * 2**20),
        name="weights",
    )(sgt, mechanism)


def circle(turns):
    half = (turns - jnp.floor(turns + 0.5)) * jnp.float32(np.pi)
    sq = half * half
    sine = jnp.float32(1.0 / 6227020800)
    for sign, power in ((-1, 39916800), (1, 362880), (-1, 5040), (1, 120), (-1, 6)):
        sine = sine * sq + jnp.float32(sign / power)
    sine = half + half * sq * sine
    cosine = jnp.float32(-1.0 / 87178291200)
    for sign, power in ((1, 479001600), (-1, 3628800), (1, 40320), (-1, 720), (1, 24), (-1, 2)):
        cosine = cosine * sq + jnp.float32(sign / power)
    cosine = cosine * sq + 1.0
    return 1.0 - 2.0 * sine * sine, 2.0 * sine * cosine


def spectra_kernel(fields_ref, weights_ref, out_ref, state, sources, sums):
    amp = fields_ref[0]
    turns = fields_ref[1] * jnp.float32(TURNS)
    rise = fields_ref[2] * jnp.float32(2 * np.pi * TURNS)
    one_c, one_s = circle(turns)
    state[0] = amp
    state[1] = jnp.zeros_like(amp)
    state[2] = amp * one_c
    state[3] = amp * one_s
    step_c, step_s = circle(turns * 2.0)
    state[4] = step_c
    state[5] = step_s
    state[8] = 2.0 * step_c
    jump_c, jump_s = circle(turns * jnp.float32(2 * STEPS))
    state[6] = jump_c
    state[7] = jump_s
    state[9] = rise * rise

    def run(turn, carry):
        base = turn * (2 * STEPS)
        for pair in range(OWNERS // 16):
            rows = slice(pair * 16, pair * 16 + 16)
            double = state[8, rows]
            rise_sq = state[9, rows]
            for parity in range(2):
                cos_now, sin_now = state[2 * parity, rows], state[2 * parity + 1, rows]
                step_c, step_s = state[4, rows], state[5, rows]
                jump_c, jump_s = state[6, rows], state[7, rows]
                state[2 * parity, rows] = cos_now * jump_c - sin_now * jump_s
                state[2 * parity + 1, rows] = sin_now * jump_c + cos_now * jump_s
                cos_next = cos_now * step_c - sin_now * step_s
                sin_next = sin_now * step_c + cos_now * step_s
                for i in range(STEPS):
                    freq = (base + (2 * i + parity)).astype(F32)
                    scale = lax.rsqrt(rise_sq * (freq * freq) + 1.0)
                    at = parity * OWNERS + pair * 16
                    sources[i, at : at + 16, 0:PTS] = (cos_now * scale).astype(BF16)
                    sources[i, at : at + 16, PTS:] = (sin_now * scale).astype(BF16)
                    if i < STEPS - 1:
                        cos_now, cos_next = cos_next, double * cos_next - cos_now
                        sin_now, sin_next = sin_next, double * sin_next - sin_now
        local = lax.rem(turn, 128 // STEPS) * STEPS
        for i in range(0, STEPS, 2):
            first = pl.multiple_of((turn * STEPS + i) * 8, 16)
            left = jnp.concatenate([weights_ref[0, pl.ds(first, 16)], weights_ref[1, pl.ds(first, 16)]], axis=1).astype(BF16)
            right = sources[i : i + 2].reshape(2 * PTS, 2 * PTS)
            product = lax.dot_general(left, right, (((1,), (1,)), ((), ())), preferred_element_type=F32)
            sums[pl.ds(local + i, 8, stride=128), :] = product[0:8, 0:128]
            sums[pl.ds(local + i + 1, 8, stride=128), :] = product[8:16, 128:256]
        return carry

    def chunk(h, carry):
        lax.fori_loop(h * (128 // STEPS), (h + 1) * (128 // STEPS), run, 0)
        for row in range(8):
            turned = jnp.transpose(sums[row * 128 : (row + 1) * 128, :])
            parity = row // 4
            out_ref[h, row] = turned[parity * OWNERS : (parity + 1) * OWNERS]
        return carry

    lax.fori_loop(0, CHUNKS, chunk, 0)


def partial_spectra(fields, weights):
    vmem = pl.BlockSpec(memory_space=pltpu.VMEM)
    return pl.pallas_call(
        spectra_kernel,
        out_shape=jax.ShapeDtypeStruct((CHUNKS, 8, OWNERS, 128), F32),
        in_specs=[vmem, vmem],
        out_specs=vmem,
        scratch_shapes=[
            pltpu.VMEM((10, OWNERS, PTS), F32),
            pltpu.VMEM((STEPS, 2 * OWNERS, 2 * PTS), BF16),
            pltpu.VMEM((8 * 128, 128), F32),
        ],
        compiler_params=pltpu.CompilerParams(vmem_limit_bytes=32 * 2**20),
        name="partial_spectra",
    )(fields, weights)


def peaks_kernel(
    start_ref, count_ref, order_ref, parts_ref, response_ref, table_ref, out_ref,
    arrived, summed, landed, limits, left, extra, best,
    send_a, recv_a, send_b, recv_b,
):
    y, b, z, j = place()
    j_peers = [(y, z * NJ + lax.rem(j + d, NJ)) for d in range(1, NJ)]
    z_peers = [(y, lax.rem(z + d, NZ) * NJ + j) for d in range(1, NZ)]
    greet(j_peers + z_peers)
    first_hop = []
    for h in range(CHUNKS):
        for d, peer in enumerate(j_peers):
            rows = pl.multiple_of(lax.rem(j + d + 1, NJ) * NZ, 8)
            copy = remote(
                parts_ref.at[h, :, pl.ds(rows, NZ), :], arrived.at[h, j],
                send_a.at[h, d], recv_a.at[h, d], peer,
            )
            copy.start()
            first_hop.append(copy)
    for h in range(CHUNKS):
        arrived[h, j] = parts_ref[h, :, pl.ds(pl.multiple_of(j * NZ, 8), NZ), :]

    def bounds(index, carry):
        slot, zz = lax.div(index, NZ), lax.rem(index, NZ)
        v = order_ref[(zz * NJ + j) * 4 + slot]
        first = start_ref[v]
        span = lax.shift_right_logical(count_ref[v] + (PTS - 1), 7)
        limits[0, pl.ds(index, 1), :] = jnp.full((1, 128), first, jnp.int32)
        limits[1, pl.ds(index, 1), :] = jnp.full((1, 128), first + span, jnp.int32)
        return carry

    lax.fori_loop(0, 4 * NZ, bounds, 0)

    second_hop = []
    for h in range(CHUNKS):
        for copy in first_hop[h * 7 : h * 7 + 7]:
            copy.wait()
        for slot in range(4):
            first = limits[0, slot * NZ : slot * NZ + NZ]
            last = limits[1, slot * NZ : slot * NZ + NZ]
            total = jnp.zeros((8, NZ, 128), F32)
            for src in range(NJ):
                at = z * NJ + src
                live = (first <= at) & (at < last)
                total = total + jnp.where(live[None], arrived[h, src], 0.0)
            for row in range(8):
                summed[h, pl.ds(slot * 8 + row, NZ, stride=32), :] = total[row]
        for d, peer in enumerate(z_peers):
            rows = pl.multiple_of(lax.rem(z + d + 1, NZ) * 32, 32)
            copy = remote(
                summed.at[h, pl.ds(rows, 32), :], landed.at[h, z], send_b.at[h, d], recv_b.at[h, d], peer
            )
            copy.start()
            second_hop.append(copy)
        landed[h, z] = summed[h, pl.ds(pl.multiple_of(z * 32, 32), 32), :]

    lane = lax.broadcasted_iota(jnp.int32, (1, 128), 1)
    sign = jnp.where(lax.rem(lane, 2) == 0, 1.0, -1.0).astype(F32)
    for h in range(CHUNKS):
        for copy in second_hop[h * 7 : h * 7 + 7]:
            copy.wait()
        total = landed[h, 0]
        for src in range(1, NZ):
            total = total + landed[h, src]
        cols = slice(h * 128, h * 128 + 128)
        for parity in range(2):
            stiff = response_ref[parity, 0, :, cols]
            friction = response_ref[parity, 1, :, cols]
            for slot in range(4):
                for c in range(2):
                    row = slot * 8 + parity * 4 + 2 * c
                    real, imag = total[row : row + 1], total[row + 1 : row + 2]
                    rows = slice((slot * 2 + c) * PAD_PERIODS, (slot * 2 + c + 1) * PAD_PERIODS)
                    for part, value in enumerate(
                        (real * stiff + imag * friction, imag * stiff - real * friction)
                    ):
                        high = value.astype(BF16)
                        left[parity, part, 0, rows, cols] = high
                        left[parity, part, 1, rows, cols] = (value - high.astype(F32)).astype(BF16)
                        if parity == 0 and part == 0:
                            if h == 0:
                                extra[rows, :] = value * sign
                            else:
                                extra[rows, :] += value * sign

    def series(parity, part, rows, cols):
        high, low = left[parity, part, 0, rows], left[parity, part, 1, rows]
        table_high, table_low = table_ref[parity, part, 0, :, cols], table_ref[parity, part, 1, :, cols]
        dot = functools.partial(jnp.dot, preferred_element_type=F32)
        return dot(high, table_high) + (dot(low, table_high) + dot(high, table_low))

    tile_rows = 2 * PAD_PERIODS

    def tile(index, carry):
        rows = pl.ds(pl.multiple_of(index * tile_rows, tile_rows), tile_rows)
        most = jnp.zeros((tile_rows, 128), F32)
        for col in range(HALF // 256):
            cols = slice(col * 256, col * 256 + 256)
            cos_even, cos_odd = series(0, 0, rows, cols), series(1, 0, rows, cols)
            sin_even, sin_odd = series(0, 1, rows, cols), series(1, 1, rows, cols)
            if col == 0:
                middle = jnp.abs(jnp.sum(extra[rows], axis=1, keepdims=True)) + jnp.abs(sin_odd[:, 0:1])
                most = jnp.maximum(most, middle)
                wide = lax.broadcasted_iota(jnp.int32, (1, 256), 1)
                sin_odd = jnp.where(wide == 0, 0.0, sin_odd)
            one = jnp.abs(cos_even + cos_odd) + jnp.abs(sin_even + sin_odd)
            two = jnp.abs(cos_even - cos_odd) + jnp.abs(sin_odd - sin_even)
            peak = jnp.maximum(one, two)
            most = jnp.maximum(most, jnp.maximum(peak[:, :128], peak[:, 128:]))
        best[rows] = most
        return carry

    lax.fori_loop(0, 4, tile, 0)
    for slot in range(4):
        pieces = []
        for c in range(2):
            at = (slot * 2 + c) * PAD_PERIODS
            turned = jnp.transpose(jnp.concatenate([best[at : at + PAD_PERIODS], jnp.zeros((128 - PAD_PERIODS, 128), F32)], axis=0))
            pieces.append(jnp.max(turned, axis=0, keepdims=True))
        moved = pltpu.roll(pieces[1], PERIODS, 1)
        row = jnp.where(lane < PERIODS, pieces[0], moved)
        out_ref[0, slot : slot + 1, :] = row[:, : 2 * PERIODS]


def owner_peaks(parts, start, count, order, response, tables):
    dma = pltpu.SemaphoreType.DMA
    smem = pl.BlockSpec(memory_space=pltpu.SMEM)
    vmem = pl.BlockSpec(memory_space=pltpu.VMEM)
    return pl.pallas_call(
        peaks_kernel,
        out_shape=jax.ShapeDtypeStruct((1, 4, 2 * PERIODS), F32),
        in_specs=[smem, smem, smem, vmem, vmem, vmem],
        out_specs=vmem,
        scratch_shapes=[
            pltpu.VMEM((CHUNKS, NJ, 8, NZ, 128), F32),
            pltpu.VMEM((CHUNKS, NZ * 32, 128), F32),
            pltpu.VMEM((CHUNKS, NZ, 32, 128), F32),
            pltpu.VMEM((2, 4 * NZ, 128), jnp.int32),
            pltpu.VMEM((2, 2, 2, ROWS, HALF), BF16),
            pltpu.VMEM((ROWS, 128), F32),
            pltpu.VMEM((ROWS, 128), F32),
            dma((CHUNKS, 7)), dma((CHUNKS, 7)), dma((CHUNKS, 7)), dma((CHUNKS, 7)),
        ],
        compiler_params=pltpu.CompilerParams(
            collective_id=1, has_side_effects=True, vmem_limit_bytes=40 * 2**20
        ),
        name="owner_peaks",
    )(start, count, order, parts, response, tables)


def solution(mesh):
    response, tables = constant_tables()

    def per_device(sgt, mechanism, slip_fields, rupture_start, point_count, owner_order):
        weights = make_weights(sgt, mechanism)
        fields = exchange_slip(slip_fields, rupture_start, point_count, owner_order)
        parts = partial_spectra(fields, weights)
        return owner_peaks(
            parts, rupture_start, point_count, owner_order, jnp.asarray(response), jnp.asarray(tables)
        )

    return jax.shard_map(
        per_device,
        mesh=mesh,
        in_specs=(
            P("site", None, None, None, "blk", None),
            P(None, "blk"),
            P("blk", None, "site"),
            P(),
            P(),
            P(),
        ),
        out_specs=P("site", "blk", None),
        check_vma=False,
    )
```

time: 461 us -> 97.4 us (0.21)
  waiting for transfers between devices: 178 us -> 0 us
  other arithmetic: 141 us -> 0 us
  Pallas kernels: 0 us -> 91.4 us
  local copies, waits for them, and re-layouts: 74.2 us -> 5.7 us
  matrix products: 24.6 us -> 0 us
  between operations: 14.9 us -> 0.13 us
  starting transfers between devices: 14 us -> 0 us
  blocking collectives: 12.2 us -> 0 us
    unnamed x2 -> x0, waiting for transfers between devices: 178 us -> none
    pallas_call x0 -> x4, Pallas kernels: none -> 91.4 us  [the longest x1 32.8 us: exchange_slip(): pl.pallas_call(slip_kernel, out_shape=jax.ShapeDtypeStruct((3, OWNERS, PT...]
    dot_general x2 -> x0, other arithmetic: 63.7 us -> none  [the longest x1 32 us: oscillator_peaks(): jnp.dot(resp_imag.reshape(-1, freq_count), sine, precision=lax.Precision....]
    mul x5 -> x0, other arithmetic: 48.7 us -> none  [the longest x3 47.1 us: source_terms(): return (scaled * jnp.cos(phase), scaled * jnp.sin(phase))]
    dot_general x2 -> x0, matrix products: 24.6 us -> none  [the longest x1 12.5 us: oscillator_peaks(): jnp.dot(resp_real.reshape(-1, freq_count), cosine, precision=lax.Precisio...]
    unnamed x22 -> x18, local copies, waits for them, and re-layouts: 29 us -> 5.7 us
    all_to_all x1 -> x0, starting transfers between devices: 14 us -> none  [per_device(): lax.all_to_all(whole_fault, 'blk', split_axis=2, concat_axis=0, tiled=True)]
    all_to_all x2 -> x0, local copies, waits for them, and re-layouts: 12.9 us -> none  [per_device(): lax.all_to_all(whole_fault, 'blk', split_axis=2, concat_axis=0, tiled=True)]
  transfers between devices with their start and end apart: 2 -> 0, of which waited for: 1 -> 0; matrix products, arithmetic and copies ran while one was open for 17% -> 0% of each run, Pallas kernels for 0% -> 0%
where the time goes in v1:
time: 97.4 us; the launch traced here: 97.2 us
  Pallas kernels  91.4 us (94%)
  local copies, waits for them, and re-layouts  5.7 us (6%)
    pallas_call x1, Pallas kernels, exchange_slip(): pl.pallas_call(slip_kernel, out_shape=jax.ShapeDtypeStruct((3, OWNERS, PT...  32.8 us
    pallas_call x1, Pallas kernels, owner_peaks(): pl.pallas_call(peaks_kernel, out_shape=jax.ShapeDtypeStruct((1, 4, 2 * PE...  32.5 us
    pallas_call x1, Pallas kernels, partial_spectra(): pl.pallas_call(spectra_kernel, out_shape=jax.ShapeDtypeStruct((CHUNKS, 8,...  23.3 us
    unnamed x18, local copies, waits for them, and re-layouts  5.7 us
    pallas_call x1, Pallas kernels, make_weights(): pl.pallas_call(weights_kernel, out_shape=jax.ShapeDtypeStruct((2, FREQ *...  2.86 us

profile of v1, /device:TPU:1, one launch (start us, length us, event | category | flops | bytes accessed | tf_op | source)
XLA Modules:
  0.0 97.2 jit_solution(3924847338369494083)
XLA Ops:
  0.0 1.6 %copy.9.slip_ref = f32[4,3,2048]{2,1,0:T(4,128)} copy(f32[4,3,2048]{2,0,1:T(4,128)} %param.10) | data formatting | bytes 196608 | tf_op args[2]
  1.6 32.8 %slip_exchange.1.fields_ref = f32[3,64,128]{2,1,0:T(8,128)} custom-call(s32[256]{0:T(256)} %start_ref.3, s32[256]{0:T(256)} %count_ref.3, s32[256]{0:T(256)} %order_ref.3, f32[4,3,2048]{2,1,0:T(4,128)} %copy.9.slip_ref), custom_call_target="tpu_custom_call" | custom-call | tf_op jit(solution)/shard_map/slip_exchange/pallas_call | solution.py:157
  34.4 0.0 copy-start
  34.4 2.8 %copy-done = bf16[1,2,6,2,128,1024]{5,4,3,2,1,0:T(8,128)(2,1)S(1)} copy-done((bf16[1,2,6,2,128,1024]{5,4,3,2,1,0:T(8,128)(2,1)S(1)}, bf16[1,2,6,2,128,1024]{5,4,3,2,1,0:T(8,128)(2,1)}, u32[]{:S(2)}) %copy-start) | copy-done | bytes 6291480
  37.2 0.0 copy-start.4
  37.2 0.7 copy-done.4
  37.9 0.0 copy-start.3
  37.9 2.9 %weights.1.weights_ref = f32[2,4096,128]{2,1,0:T(8,128)S(1)} custom-call(bf16[1,2,6,2,128,1024]{5,4,3,2,1,0:T(8,128)(2,1)S(1)} %copy-done, f32[6,128]{1,0:T(8,128)S(1)} %copy-done.4), custom_call_target="tpu_custom_call" | custom-call | tf_op jit(solution)/shard_map/weights/pallas_call | solution.py:201
  40.7 0.0 copy-done.3
  40.8 0.0 copy-start.1
  40.8 0.0 copy-start.2
  40.8 0.0 copy-start.5
  40.8 0.0 copy-start.6
  40.8 0.0 copy-start.7
  40.8 23.3 %partial_spectra.1.parts_ref = f32[4,8,64,128]{3,2,1,0:T(8,128)S(1)} custom-call(f32[3,64,128]{2,1,0:T(8,128)S(1)} %copy-done.3, f32[2,4096,128]{2,1,0:T(8,128)S(1)} %weights.1.weights_ref), custom_call_target="tpu_custom_call" | custom-call | tf_op jit(solution)/shard_map/partial_spectra/pallas_call | solution.py:290
  64.1 0.0 copy-done.1
  64.1 0.0 copy-done.2
  64.1 0.0 copy-done.5
  64.1 0.0 copy-done.6
  64.1 0.0 copy-done.7
  64.1 32.5 %owner_peaks.1 = f32[1,4,88]{2,1,0:T(4,128)S(1)} custom-call(s32[256]{0:T(256)S(1)} %copy-done.5, s32[256]{0:T(256)S(1)} %copy-done.6, s32[256]{0:T(256)S(1)} %copy-done.7, f32[4,8,64,128]{3,2,1,0:T(8,128)S(1)} %partial_spectra.1.parts_ref, f32[2,2,48,512]{3,2,1,0:T(8,128)S(1)} %copy-done.2, bf16[2,2,2,512,512]{4,3,2,1,0:T(8,128)(2,1)S(1)} %copy-done.1), custom_call_target="tpu_custom_call" | custom-call | tf_op jit(solution)/shard_map/owner_peaks/pallas_call | solution.py:433
  96.6 0.6 copy.11
Async XLA Ops:
  34.4 2.8 %copy-start = (bf16[1,2,6,2,128,1024]{5,4,3,2,1,0:T(8,128)(2,1)S(1)}, bf16[1,2,6,2,128,1024]{5,4,3,2,1,0:T(8,128)(2,1)}, u32[]{:S(2)}) copy-start(bf16[1,2,6,2,128,1024]{5,4,3,2,1,0:T(8,128)(2,1)} %sgt_ref.1) | copy-start | bytes 18874372
  37.2 0.7 copy-start.4
  37.9 2.9 %copy-start.3 = (f32[3,64,128]{2,1,0:T(8,128)S(1)}, f32[3,64,128]{2,1,0:T(8,128)}, u32[]{:S(2)}) copy-start(f32[3,64,128]{2,1,0:T(8,128)} %slip_exchange.1.fields_ref) | copy-start | bytes 294916
  40.8 23.3 %copy-start.1 = (bf16[2,2,2,512,512]{4,3,2,1,0:T(8,128)(2,1)S(1)}, bf16[2,2,2,512,512]{4,3,2,1,0:T(8,128)(2,1)}, u32[]{:S(2)}) copy-start(bf16[2,2,2,512,512]{4,3,2,1,0:T(8,128)(2,1)} %constant.5.clone.table_ref) | copy-start | bytes 12582916
  40.8 23.3 %copy-start.2 = (f32[2,2,48,512]{3,2,1,0:T(8,128)S(1)}, f32[2,2,48,512]{3,2,1,0:T(8,128)}, u32[]{:S(2)}) copy-start(f32[2,2,48,512]{3,2,1,0:T(8,128)} %constant.4.clone.response_ref) | copy-start | bytes 1179652
  40.8 23.3 %copy-start.5 = (s32[256]{0:T(256)S(1)}, s32[256]{0:T(256)}, u32[]{:S(2)}) copy-start(s32[256]{0:T(256)} %start_ref.3) | copy-start | bytes 3076
  40.8 23.3 %copy-start.6 = (s32[256]{0:T(256)S(1)}, s32[256]{0:T(256)}, u32[]{:S(2)}) copy-start(s32[256]{0:T(256)} %count_ref.3) | copy-start | bytes 3076
  40.8 23.3 %copy-start.7 = (s32[256]{0:T(256)S(1)}, s32[256]{0:T(256)}, u32[]{:S(2)}) copy-start(s32[256]{0:T(256)} %order_ref.3) | copy-start | bytes 3076

commit v2 on v1

v2 whole, which is shorter than its diff:
```python
import functools

import jax
import jax.numpy as jnp
import ml_dtypes
import numpy as np
from jax import lax
from jax.experimental import pallas as pl
from jax.experimental.pallas import tpu as pltpu
from jax.sharding import PartitionSpec as P

MESH = pl.DeviceIdType.MESH
FREQ = 1024
PERIODS = 44
PAD_PERIODS = 48
PTS = 128
SITES = 4
NZ = 8
NJ = 8
OWNERS = NZ * NJ
CHUNKS = 4
STEPS = 32
ROWS = 8 * PAD_PERIODS
HALF = FREQ // 2
DT = 0.1
DAMPING = 0.05
TURNS = 1.0 / (2 * FREQ * DT)
F32 = jnp.float32
BF16 = jnp.bfloat16


def split_table(table):
    high = table.astype(ml_dtypes.bfloat16)
    low = (table - high.astype(np.float64)).astype(ml_dtypes.bfloat16)
    return high, low


def constant_tables():
    freq = np.arange(FREQ)
    omega = 2 * np.pi * freq * TURNS
    factor = np.where(freq == 0, 1.0, 2.0) / FREQ
    natural = 2 * np.pi / (0.2 * 50.0 ** (np.arange(PERIODS) / (PERIODS - 1)))
    stiffness = natural[:, None] ** 2 - omega[None] ** 2
    friction = 2 * DAMPING * natural[:, None] * omega[None]
    number = np.where(freq == 0, 2.0**-10, freq)
    gain = factor[None] / number[None] * natural[:, None] ** 2 / (stiffness**2 + friction**2)
    response = np.zeros((2, 2, PAD_PERIODS, HALF), np.float32)
    for parity in range(2):
        response[parity, 0, :PERIODS] = (gain * stiffness)[:, parity::2]
        response[parity, 1, :PERIODS] = (gain * friction)[:, parity::2]
    sample = np.arange(HALF)
    tables = np.zeros((2, 2, 2, HALF, HALF), ml_dtypes.bfloat16)
    for parity in range(2):
        ids = freq[parity::2]
        angle = 2 * np.pi * ((ids[:, None] * sample[None]) % (2 * FREQ)) / (2 * FREQ)
        tables[parity, 0, 0], tables[parity, 0, 1] = split_table(np.cos(angle))
        sine = np.sin(angle)
        if parity == 1:
            sine[:, 0] = np.where(np.arange(HALF) % 2 == 0, 1.0, -1.0)
        tables[parity, 1, 0], tables[parity, 1, 1] = split_table(sine)
    return response, tables, (1.0 / number**2).astype(np.float32)


def place():
    y = lax.axis_index("site")
    b = lax.axis_index("blk")
    return y, b, lax.div(b, NJ), lax.rem(b, NJ)


def greet(peers):
    barrier = pltpu.get_barrier_semaphore()
    for peer in peers:
        pl.semaphore_signal(barrier, inc=1, device_id=peer, device_id_type=MESH)
    pl.semaphore_wait(barrier, len(peers))


def remote(src, dst, send, recv, peer):
    return pltpu.make_async_remote_copy(
        src_ref=src, dst_ref=dst, send_sem=send, recv_sem=recv, device_id=peer, device_id_type=MESH
    )


def fields_kernel(
    start_ref, count_ref, order_ref, slip_ref, mech_ref, sgt_ref,
    fields_ref, weights_ref, limits_ref,
    mine, plane, block, chosen, points, mech_wide, sgt,
    send_a, recv_a, send_b, recv_b, send_c, recv_c, load_sem,
):
    y, b, z, j = place()
    loads = [pltpu.make_async_copy(sgt_ref.at[0, c], sgt.at[c], load_sem.at[c]) for c in range(2)]
    for load in loads:
        load.start()
    y_peers = [(lax.rem(y + d, SITES), b) for d in range(1, SITES)]
    z_peers = [(y, lax.rem(z + d, NZ) * NJ + j) for d in range(1, NZ)]
    turns = [(dy, dj) for dj in range(NJ) for dy in range(SITES) if dy or dj]
    plane_peers = [(lax.rem(y + dy, SITES), z * NJ + lax.rem(j + dj, NJ)) for dy, dj in turns]
    greet(plane_peers + z_peers)
    for v in range(4):
        for zz in range(2):
            for jj in range(NJ):
                at = (zz * NJ + jj) * PTS
                for k in range(3):
                    mine[v, jj, zz, k] = slip_ref[k, v : v + 1, at : at + PTS]
    copies = []
    for d, peer in enumerate(plane_peers):
        copy = remote(
            mine.at[peer[0], lax.rem(peer[1], NJ)], plane.at[j, pl.ds(2 * y, 2)], send_a.at[d], recv_a.at[d], peer
        )
        copy.start()
        copies.append(copy)
    plane[j, pl.ds(2 * y, 2)] = mine[y, j]

    turned = jnp.transpose(jnp.concatenate([mech_ref[...], jnp.zeros((2, PTS), F32)], axis=0))
    for k in range(6):
        mech_wide[k] = jnp.broadcast_to(turned[:, k : k + 1], (PTS, PTS))

    def weights_of(c):
        def tile(step, carry):
            at = pl.multiple_of(step * PTS, PTS)
            for part in range(2):
                total = mech_wide[0] * sgt[c, 0, part, :, pl.ds(at, PTS)].astype(F32)
                for k in range(1, 6):
                    total = total + mech_wide[k] * sgt[c, k, part, :, pl.ds(at, PTS)].astype(F32)
                turned = jnp.transpose(total)
                rows = at * 4 + 2 * c
                weights_ref[part, pl.ds(rows, PTS, stride=4), :] = turned
                weights_ref[1 - part, pl.ds(rows + 1, PTS, stride=4), :] = turned if part else -turned
            return carry

        lax.fori_loop(0, FREQ // PTS, tile, 0)

    loads[0].wait()
    weights_of(0)
    for copy in copies:
        copy.wait()
    copies = []
    for d, peer in enumerate(z_peers):
        target = lax.rem(z + d + 1, NZ)
        copy = remote(plane.at[:, target], block.at[y, z], send_b.at[d], recv_b.at[d], peer)
        copy.start()
        copies.append(copy)
    block[y, z] = plane[:, z]
    spread = []

    def forward(turn, row):
        for d, peer in enumerate(y_peers):
            copy = remote(block.at[y, row], block.at[y, row], send_c.at[turn, d], recv_c.at[turn, d], peer)
            copy.start()
            spread.append(copy)

    forward(0, z)

    def choose(row, carry):
        owner = lax.rem(row, NZ) * NJ + lax.div(row, NZ)
        best = jnp.int32(0)
        active = jnp.int32(0)
        for slot in range(4):
            v = order_ref[owner * 4 + slot]
            first = start_ref[v]
            remaining = count_ref[v] - (b - first) * PTS
            live = (first <= b) & (remaining > 0)
            best = jnp.where(live, v, best)
            active = jnp.where(live, remaining, active)
        chosen[row] = best
        points[row] = active
        return carry

    lax.fori_loop(0, OWNERS, choose, 0)
    for d, copy in enumerate(copies):
        copy.wait_recv()
        forward(d + 1, lax.rem(z + NZ - d - 1, NZ))

    def bounds(index, carry):
        slot, zz = lax.div(index, NZ), lax.rem(index, NZ)
        v = order_ref[(zz * NJ + j) * 4 + slot]
        first = start_ref[v]
        span = lax.shift_right_logical(count_ref[v] + (PTS - 1), 7)
        limits_ref[0, pl.ds(index, 1), :] = jnp.full((1, 128), first, jnp.int32)
        limits_ref[1, pl.ds(index, 1), :] = jnp.full((1, 128), first + span, jnp.int32)
        return carry

    lax.fori_loop(0, 4 * NZ, bounds, 0)
    loads[1].wait()
    weights_of(1)
    for copy in copies:
        copy.wait_send()
    for copy in spread:
        copy.wait()

    lane = lax.broadcasted_iota(jnp.int32, (1, PTS), 1)

    def select(row, carry):
        v = chosen[row]
        at = (v & 3, lax.shift_right_logical(v, 5), lax.shift_right_logical(v, 2) & 7)
        fields_ref[0, pl.ds(row, 1), :] = jnp.where(lane < points[row], block[at + (0,)], 0.0)
        fields_ref[1, pl.ds(row, 1), :] = block[at + (1,)]
        fields_ref[2, pl.ds(row, 1), :] = block[at + (2,)]
        return carry

    lax.fori_loop(0, OWNERS, select, 0)


def fields_and_weights(sgt, mechanism, slip, start, count, order):
    dma = pltpu.SemaphoreType.DMA
    smem = pl.BlockSpec(memory_space=pltpu.SMEM)
    vmem = pl.BlockSpec(memory_space=pltpu.VMEM)
    return pl.pallas_call(
        fields_kernel,
        out_shape=(
            jax.ShapeDtypeStruct((3, OWNERS, PTS), F32),
            jax.ShapeDtypeStruct((2, FREQ * 4, PTS), F32),
            jax.ShapeDtypeStruct((2, 4 * NZ, 128), jnp.int32),
        ),
        in_specs=[smem, smem, smem, vmem, vmem, pl.BlockSpec(memory_space=pl.ANY)],
        out_specs=(vmem, vmem, vmem),
        scratch_shapes=[
            pltpu.VMEM((4, NJ, 2, 3, 1, PTS), F32),
            pltpu.VMEM((NJ, NZ, 3, 1, PTS), F32),
            pltpu.VMEM((4, NZ, NJ, 3, 1, PTS), F32),
            pltpu.SMEM((OWNERS,), jnp.int32),
            pltpu.SMEM((OWNERS,), jnp.int32),
            pltpu.VMEM((6, PTS, PTS), F32),
            pltpu.VMEM((2, 6, 2, PTS, FREQ), BF16),
            dma((31,)), dma((31,)), dma((7,)), dma((7,)), dma((8, 3)), dma((8, 3)), dma((2,)),
        ],
        compiler_params=pltpu.CompilerParams(
            collective_id=0, has_side_effects=True, vmem_limit_bytes=40 * 2**20
        ),
        name="fields_and_weights",
    )(start, count, order, jnp.transpose(slip, (1, 0, 2)), mechanism, sgt)


def circle(turns):
    half = (turns - jnp.floor(turns + 0.5)) * jnp.float32(np.pi)
    sq = half * half
    sine = jnp.float32(1.0 / 6227020800)
    for sign, power in ((-1, 39916800), (1, 362880), (-1, 5040), (1, 120), (-1, 6)):
        sine = sine * sq + jnp.float32(sign / power)
    sine = half + half * sq * sine
    cosine = jnp.float32(-1.0 / 87178291200)
    for sign, power in ((1, 479001600), (-1, 3628800), (1, 40320), (-1, 720), (1, 24), (-1, 2)):
        cosine = cosine * sq + jnp.float32(sign / power)
    cosine = cosine * sq + 1.0
    return 1.0 - 2.0 * sine * sine, 2.0 * sine * cosine


def peaks_kernel(
    inverse_ref, fields_ref, weights_ref, limits_ref, response_ref, table_ref, out_ref,
    state, source_cos, source_sin, sums, parts, arrived, summed, landed, left, extra, total_series, best,
    send_a, recv_a, send_b, recv_b,
):
    y, b, z, j = place()
    j_peers = [(y, z * NJ + lax.rem(j + d, NJ)) for d in range(1, NJ)]
    z_peers = [(y, lax.rem(z + d, NZ) * NJ + j) for d in range(1, NZ)]
    barrier = pltpu.get_barrier_semaphore()
    for peer in j_peers + z_peers:
        pl.semaphore_signal(barrier, inc=1, device_id=peer, device_id_type=MESH)

    amp = fields_ref[0]
    turns = fields_ref[1] * jnp.float32(TURNS)
    rise = fields_ref[2] * jnp.float32(2 * np.pi * TURNS)
    one_c, one_s = circle(turns)
    state[0] = amp
    state[1] = jnp.zeros_like(amp)
    state[2] = amp * one_c
    state[3] = amp * one_s
    step_c, step_s = circle(turns * 2.0)
    state[4] = step_c
    state[5] = step_s
    state[8] = 2.0 * step_c
    jump_c, jump_s = circle(turns * jnp.float32(2 * STEPS))
    state[6] = jump_c
    state[7] = jump_s
    state[9] = rise * rise

    def run(turn, carry):
        base = turn * (2 * STEPS)
        for pair in range(OWNERS // 16):
            rows = slice(pair * 16, pair * 16 + 16)
            double = state[8, rows]
            rise_sq = state[9, rows]
            for parity in range(2):
                cos_now, sin_now = state[2 * parity, rows], state[2 * parity + 1, rows]
                step_c, step_s = state[4, rows], state[5, rows]
                jump_c, jump_s = state[6, rows], state[7, rows]
                state[2 * parity, rows] = cos_now * jump_c - sin_now * jump_s
                state[2 * parity + 1, rows] = sin_now * jump_c + cos_now * jump_s
                cos_next = cos_now * step_c - sin_now * step_s
                sin_next = sin_now * step_c + cos_now * step_s
                at = parity * OWNERS + pair * 16
                for i in range(STEPS):
                    scale = lax.rsqrt(rise_sq + inverse_ref[base + (2 * i + parity)])
                    source_cos[i, at : at + 16, :] = (cos_now * scale).astype(BF16)
                    source_sin[i, at : at + 16, :] = (sin_now * scale).astype(BF16)
                    if i < STEPS - 1:
                        cos_now, cos_next = cos_next, double * cos_next - cos_now
                        sin_now, sin_next = sin_next, double * sin_next - sin_now
        local = lax.rem(turn, 128 // STEPS) * STEPS
        for i in range(0, STEPS, 2):
            first = pl.multiple_of((turn * STEPS + i) * 8, 16)
            lhs = jnp.concatenate([weights_ref[0, pl.ds(first, 16)], weights_ref[1, pl.ds(first, 16)]], axis=1).astype(BF16)
            rhs = jnp.concatenate(
                [source_cos[i : i + 2].reshape(2 * PTS, PTS), source_sin[i : i + 2].reshape(2 * PTS, PTS)], axis=1
            )
            product = lax.dot_general(lhs, rhs, (((1,), (1,)), ((), ())), preferred_element_type=F32)
            sums[pl.ds(local + i, 8, stride=128), :] = product[0:8, 0:128]
            sums[pl.ds(local + i + 1, 8, stride=128), :] = product[8:16, 128:256]
        return carry

    def send_parts(h):
        for row in range(8):
            turned = jnp.transpose(sums[row * 128 : (row + 1) * 128, :])
            parity = row // 4
            parts[h, row] = turned[parity * OWNERS : (parity + 1) * OWNERS]
        copies = []
        for d, peer in enumerate(j_peers):
            rows = pl.multiple_of(lax.rem(j + d + 1, NJ) * NZ, 8)
            copy = remote(
                parts.at[h, :, pl.ds(rows, NZ), :], arrived.at[h, j], send_a.at[h, d], recv_a.at[h, d], peer
            )
            copy.start()
            copies.append(copy)
        arrived[h, j] = parts[h, :, pl.ds(pl.multiple_of(j * NZ, 8), NZ), :]
        return copies

    def send_sums(h, copies):
        for copy in copies:
            copy.wait()
        for slot in range(4):
            first = limits_ref[0, slot * NZ : slot * NZ + NZ]
            last = limits_ref[1, slot * NZ : slot * NZ + NZ]
            total = jnp.zeros((8, NZ, 128), F32)
            for src in range(NJ):
                at = z * NJ + src
                live = (first <= at) & (at < last)
                total = total + jnp.where(live[None], arrived[h, src], 0.0)
            for row in range(8):
                summed[h, pl.ds(slot * 8 + row, NZ, stride=32), :] = total[row]
        copies = []
        for d, peer in enumerate(z_peers):
            rows = pl.multiple_of(lax.rem(z + d + 1, NZ) * 32, 32)
            copy = remote(
                summed.at[h, pl.ds(rows, 32), :], landed.at[h, z], send_b.at[h, d], recv_b.at[h, d], peer
            )
            copy.start()
            copies.append(copy)
        landed[h, z] = summed[h, pl.ds(pl.multiple_of(z * 32, 32), 32), :]
        return copies

    lane = lax.broadcasted_iota(jnp.int32, (1, 128), 1)
    sign = jnp.where(lax.rem(lane, 2) == 0, 1.0, -1.0).astype(F32)

    def respond(h, copies):
        for copy in copies:
            copy.wait()
        total = landed[h, 0]
        for src in range(1, NZ):
            total = total + landed[h, src]
        cols = slice(h * 128, h * 128 + 128)
        for parity in range(2):
            stiff = response_ref[parity, 0, :, cols]
            friction = response_ref[parity, 1, :, cols]
            for slot in range(4):
                for c in range(2):
                    row = slot * 8 + parity * 4 + 2 * c
                    real, imag = total[row : row + 1], total[row + 1 : row + 2]
                    rows = slice((slot * 2 + c) * PAD_PERIODS, (slot * 2 + c + 1) * PAD_PERIODS)
                    for part, value in enumerate(
                        (real * stiff + imag * friction, imag * stiff - real * friction)
                    ):
                        high = value.astype(BF16)
                        left[h, parity, part, rows, 0:128] = high
                        left[h, parity, part, rows, 128:256] = (value - high.astype(F32)).astype(BF16)
                        if parity == 0 and part == 0:
                            if h == 0:
                                extra[rows, :] = value * sign
                            else:
                                extra[rows, :] += value * sign

    tile_rows = 2 * PAD_PERIODS

    def series(h, parity, part, rows, cols):
        both = left[h, parity, part, rows]
        at = slice(h * 128, h * 128 + 128)
        high, low = table_ref[parity, part, 0, at, cols], table_ref[parity, part, 1, at, cols]
        dot = functools.partial(jnp.dot, preferred_element_type=F32)
        value = dot(both, jnp.concatenate([high, high], axis=0)) + dot(both[:, :128], low)
        return value if h == 0 else value + total_series[parity, part, rows, cols]

    def add_series(h):
        def tile(index, carry):
            rows = pl.ds(pl.multiple_of(index * tile_rows, tile_rows), tile_rows)
            for col in range(HALF // 256):
                cols = slice(col * 256, col * 256 + 256)
                for parity in range(2):
                    for part in range(2):
                        total_series[parity, part, rows, cols] = series(h, parity, part, rows, cols)
            return carry

        lax.fori_loop(0, 4, tile, 0)

    def last_series(h):
        def tile(index, carry):
            rows = pl.ds(pl.multiple_of(index * tile_rows, tile_rows), tile_rows)
            most = jnp.zeros((tile_rows, 128), F32)
            for col in range(HALF // 256):
                cols = slice(col * 256, col * 256 + 256)
                cos_even, cos_odd = series(h, 0, 0, rows, cols), series(h, 1, 0, rows, cols)
                sin_even, sin_odd = series(h, 0, 1, rows, cols), series(h, 1, 1, rows, cols)
                if col == 0:
                    middle = jnp.abs(jnp.sum(extra[rows], axis=1, keepdims=True)) + jnp.abs(sin_odd[:, 0:1])
                    most = jnp.maximum(most, middle)
                    wide = lax.broadcasted_iota(jnp.int32, (1, 256), 1)
                    sin_odd = jnp.where(wide == 0, 0.0, sin_odd)
                one = jnp.abs(cos_even + cos_odd) + jnp.abs(sin_even + sin_odd)
                two = jnp.abs(cos_even - cos_odd) + jnp.abs(sin_odd - sin_even)
                peak = jnp.maximum(one, two)
                most = jnp.maximum(most, jnp.maximum(peak[:, :128], peak[:, 128:]))
            best[rows] = most
            return carry

        lax.fori_loop(0, 4, tile, 0)

    turns_each = 128 // STEPS
    first_hop, second_hop = {}, {}
    for h in range(CHUNKS):
        lax.fori_loop(h * turns_each, (h + 1) * turns_each, run, 0)
        if h == 0:
            pl.semaphore_wait(barrier, len(j_peers) + len(z_peers))
        first_hop[h] = send_parts(h)
        if h >= 1:
            second_hop[h - 1] = send_sums(h - 1, first_hop[h - 1])
        if h >= 2:
            respond(h - 2, second_hop[h - 2])
    for h in range(2):
        add_series(h)
    second_hop[3] = send_sums(3, first_hop[3])
    respond(2, second_hop[2])
    add_series(2)
    respond(3, second_hop[3])
    last_series(3)

    for slot in range(4):
        pieces = []
        for c in range(2):
            at = (slot * 2 + c) * PAD_PERIODS
            turned = jnp.transpose(jnp.concatenate([best[at : at + PAD_PERIODS], jnp.zeros((128 - PAD_PERIODS, 128), F32)], axis=0))
            pieces.append(jnp.max(turned, axis=0, keepdims=True))
        moved = pltpu.roll(pieces[1], PERIODS, 1)
        row = jnp.where(lane < PERIODS, pieces[0], moved)
        out_ref[0, slot : slot + 1, :] = row[:, : 2 * PERIODS]


def owner_peaks(inverse, fields, weights, limits, response, tables):
    dma = pltpu.SemaphoreType.DMA
    vmem = pl.BlockSpec(memory_space=pltpu.VMEM)
    return pl.pallas_call(
        peaks_kernel,
        out_shape=jax.ShapeDtypeStruct((1, 4, 2 * PERIODS), F32),
        in_specs=[pl.BlockSpec(memory_space=pltpu.SMEM)] + [vmem] * 5,
        out_specs=vmem,
        scratch_shapes=[
            pltpu.VMEM((10, OWNERS, PTS), F32),
            pltpu.VMEM((STEPS, 2 * OWNERS, PTS), BF16),
            pltpu.VMEM((STEPS, 2 * OWNERS, PTS), BF16),
            pltpu.VMEM((8 * 128, 128), F32),
            pltpu.VMEM((CHUNKS, 8, OWNERS, 128), F32),
            pltpu.VMEM((CHUNKS, NJ, 8, NZ, 128), F32),
            pltpu.VMEM((CHUNKS, NZ * 32, 128), F32),
            pltpu.VMEM((CHUNKS, NZ, 32, 128), F32),
            pltpu.VMEM((CHUNKS, 2, 2, ROWS, 256), BF16),
            pltpu.VMEM((ROWS, 128), F32),
            pltpu.VMEM((2, 2, ROWS, HALF), F32),
            pltpu.VMEM((ROWS, 128), F32),
            dma((CHUNKS, 7)), dma((CHUNKS, 7)), dma((CHUNKS, 7)), dma((CHUNKS, 7)),
        ],
        compiler_params=pltpu.CompilerParams(
            collective_id=1, has_side_effects=True, vmem_limit_bytes=48 * 2**20
        ),
        name="owner_peaks",
    )(inverse, fields, weights, limits, response, tables)


def solution(mesh):
    response, tables, inverse = constant_tables()

    def per_device(sgt, mechanism, slip_fields, rupture_start, point_count, owner_order):
        fields, weights, limits = fields_and_weights(
            sgt, mechanism, slip_fields, rupture_start, point_count, owner_order
        )
        return owner_peaks(
            jnp.asarray(inverse), fields, weights, limits, jnp.asarray(response), jnp.asarray(tables)
        )

    return jax.shard_map(
        per_device,
        mesh=mesh,
        in_specs=(
            P("site", None, None, None, "blk", None),
            P(None, "blk"),
            P("blk", None, "site"),
            P(),
            P(),
            P(),
        ),
        out_specs=P("site", "blk", None),
        check_vma=False,
    )
```

time: 97.4 us -> 72.6 us (0.75)
  Pallas kernels: 91.4 us -> 65.3 us
  local copies, waits for them, and re-layouts: 5.7 us -> 6.99 us
    pallas_call x3 -> x1, Pallas kernels: 58.9 us -> 26.7 us  [fields_and_weights(): pl.pallas_call(fields_kernel, out_shape=(jax.ShapeDtypeStruct((3, OWNERS,...]
    pallas_call x1, Pallas kernels: 32.5 us -> 38.6 us  [owner_peaks(): pl.pallas_call(peaks_kernel, out_shape=jax.ShapeDtypeStruct((1, 4, 2 * PE...]
    unnamed x18 -> x17, local copies, waits for them, and re-layouts: 5.7 us -> 6.99 us
where the time goes in v2:
time: 72.6 us; the launch traced here: 72.3 us
  Pallas kernels  65.3 us (90%)
  local copies, waits for them, and re-layouts  6.99 us (10%)
    pallas_call x1, Pallas kernels, owner_peaks(): pl.pallas_call(peaks_kernel, out_shape=jax.ShapeDtypeStruct((1, 4, 2 * PE...  38.6 us
    pallas_call x1, Pallas kernels, fields_and_weights(): pl.pallas_call(fields_kernel, out_shape=(jax.ShapeDtypeStruct((3, OWNERS,...  26.7 us
    unnamed x17, local copies, waits for them, and re-layouts  6.99 us

profile of v2, /device:TPU:1, one launch (start us, length us, event | category | flops | bytes accessed | tf_op | source)
XLA Modules:
  0.0 72.3 jit_solution(2855445684103152294)
XLA Ops:
  0.0 0.0 copy-start
  0.0 2.8 %copy-done = bf16[1,2,6,2,128,1024]{5,4,3,2,1,0:T(8,128)(2,1)S(1)} copy-done((bf16[1,2,6,2,128,1024]{5,4,3,2,1,0:T(8,128)(2,1)S(1)}, bf16[1,2,6,2,128,1024]{5,4,3,2,1,0:T(8,128)(2,1)}, u32[]{:S(2)}) %copy-start) | copy-done | bytes 6291480
  2.8 0.0 copy-start.2
  2.8 0.9 %copy-done.2 = f32[4,3,2048]{2,0,1:T(4,128)S(1)} copy-done((f32[4,3,2048]{2,0,1:T(4,128)S(1)}, f32[4,3,2048]{2,0,1:T(4,128)}, u32[]{:S(2)}) %copy-start.2) | copy-done | bytes 98328
  3.7 0.0 copy-start.4
  3.7 0.7 copy-done.4
  4.4 0.0 copy-start.5
  4.4 0.7 copy-done.5
  5.0 0.0 copy-start.6
  5.0 0.7 copy-done.6
  5.7 0.0 copy-start.7
  5.7 0.7 copy-done.7
  6.4 0.0 copy-start.1
  6.4 0.0 copy-start.3
  6.4 26.7 %fields_and_weights.1 = (f32[3,64,128]{2,1,0:T(8,128)S(1)}, f32[2,4096,128]{2,1,0:T(8,128)S(1)}, s32[2,32,128]{2,1,0:T(8,128)S(1)}) custom-call(s32[256]{0:T(256)S(1)} %copy-done.5, s32[256]{0:T(256)S(1)} %copy-done.6, s32[256]{0:T(256)S(1)} %copy-done.7, f32[3,4,2048]{2,1,0:T(4,128)S(1)} %bitcast.1, f32[6,128]{1,0:T(8,128)S(1)} %copy-done.4, ...), custom_call_target="tpu_custom_call" | custom-call | tf_op jit(solution)/shard_map/fields_and_weights/pallas_call | solution.py:207
  33.1 0.0 copy-done.1
  33.1 0.0 copy-done.3
  33.1 38.6 %owner_peaks.1 = f32[1,4,88]{2,1,0:T(4,128)S(1)} custom-call(f32[1024]{0:T(1024)S(1)} %copy-done.3, f32[3,64,128]{2,1,0:T(8,128)S(1)} %get-tuple-element.8.fields_ref, f32[2,4096,128]{2,1,0:T(8,128)S(1)} %get-tuple-element.9.weights_ref, s32[2,32,128]{2,1,0:T(8,128)S(1)} %get-tuple-element.10.limits_ref, f32[2,2,48,512]{3,2,1,0:T(8,128)S(1)} %copy-done.1, ...), custom_call_target="tpu_custom_call" | custom-call | tf_op jit(solution)/shard_map/owner_peaks/pallas_call | solution.py:457
  71.8 0.6 copy.11
Async XLA Ops:
  0.0 2.8 %copy-start = (bf16[1,2,6,2,128,1024]{5,4,3,2,1,0:T(8,128)(2,1)S(1)}, bf16[1,2,6,2,128,1024]{5,4,3,2,1,0:T(8,128)(2,1)}, u32[]{:S(2)}) copy-start(bf16[1,2,6,2,128,1024]{5,4,3,2,1,0:T(8,128)(2,1)} %sgt_ref.1) | copy-start | bytes 18874372
  2.8 0.9 %copy-start.2 = (f32[4,3,2048]{2,0,1:T(4,128)S(1)}, f32[4,3,2048]{2,0,1:T(4,128)}, u32[]{:S(2)}) copy-start(f32[4,3,2048]{2,0,1:T(4,128)} %param.11) | copy-start | bytes 294916
  3.7 0.7 copy-start.4
  4.4 0.7 copy-start.5
  5.0 0.7 copy-start.6
  5.7 0.7 copy-start.7
  6.4 26.7 %copy-start.1 = (f32[2,2,48,512]{3,2,1,0:T(8,128)S(1)}, f32[2,2,48,512]{3,2,1,0:T(8,128)}, u32[]{:S(2)}) copy-start(f32[2,2,48,512]{3,2,1,0:T(8,128)} %constant.7.clone.response_ref) | copy-start | bytes 1179652
  6.4 26.7 %copy-start.3 = (f32[1024]{0:T(1024)S(1)}, f32[1024]{0:T(1024)}, u32[]{:S(2)}) copy-start(f32[1024]{0:T(1024)} %constant.6.clone.inverse_ref) | copy-start | bytes 12292

commit v3 on v2

--- a/solution.py
+++ b/solution.py
@@ -67,40 +67,57 @@
     return y, b, lax.div(b, NJ), lax.rem(b, NJ)
 
 
-def greet(peers):
-    barrier = pltpu.get_barrier_semaphore()
-    for peer in peers:
-        pl.semaphore_signal(barrier, inc=1, device_id=peer, device_id_type=MESH)
-    pl.semaphore_wait(barrier, len(peers))
-
-
 def remote(src, dst, send, recv, peer):
     return pltpu.make_async_remote_copy(
         src_ref=src, dst_ref=dst, send_sem=send, recv_sem=recv, device_id=peer, device_id_type=MESH
     )
 
 
-def fields_kernel(
-    start_ref, count_ref, order_ref, slip_ref, mech_ref, sgt_ref,
-    fields_ref, weights_ref, limits_ref,
-    mine, plane, block, chosen, points, mech_wide, sgt,
-    send_a, recv_a, send_b, recv_b, send_c, recv_c, load_sem,
+def circle(turns):
+    half = (turns - jnp.floor(turns + 0.5)) * jnp.float32(np.pi)
+    sq = half * half
+    sine = jnp.float32(1.0 / 6227020800)
+    for sign, power in ((-1, 39916800), (1, 362880), (-1, 5040), (1, 120), (-1, 6)):
+        sine = sine * sq + jnp.float32(sign / power)
+    sine = half + half * sq * sine
+    cosine = jnp.float32(-1.0 / 87178291200)
+    for sign, power in ((1, 479001600), (-1, 3628800), (1, 40320), (-1, 720), (1, 24), (-1, 2)):
+        cosine = cosine * sq + jnp.float32(sign / power)
+    cosine = cosine * sq + 1.0
+    return 1.0 - 2.0 * sine * sine, 2.0 * sine * cosine
+
+
+def kernel(
+    start_ref, count_ref, order_ref, inverse_ref, slip_hbm, mech_hbm, sgt_hbm, response_hbm, table_hbm, out_ref,
+    slip_ref, mech_ref, sgt, response_ref, table_ref,
+    mine, plane, block, chosen, points, mech_wide, turning, weights, limits_ref, fields_ref,
+    state, source_cos, source_sin, parts, arrived, summed, landed, left, extra, total_series, best,
+    load_sem, send_a, recv_a, send_b, recv_b, send_c, recv_c, send_d, recv_d, send_e, recv_e,
 ):
     y, b, z, j = place()
-    loads = [pltpu.make_async_copy(sgt_ref.at[0, c], sgt.at[c], load_sem.at[c]) for c in range(2)]
-    for load in loads:
+    slip_load = pltpu.make_async_copy(slip_hbm, slip_ref, load_sem.at[2])
+    mech_load = pltpu.make_async_copy(mech_hbm, mech_ref, load_sem.at[3])
+    loads = [pltpu.make_async_copy(sgt_hbm.at[0, c], sgt.at[c], load_sem.at[c]) for c in range(2)]
+    response_load = pltpu.make_async_copy(response_hbm, response_ref, load_sem.at[4])
+    table_load = pltpu.make_async_copy(table_hbm, table_ref, load_sem.at[5])
+    for load in (slip_load, mech_load, *loads, response_load, table_load):
         load.start()
     y_peers = [(lax.rem(y + d, SITES), b) for d in range(1, SITES)]
+    j_peers = [(y, z * NJ + lax.rem(j + d, NJ)) for d in range(1, NJ)]
     z_peers = [(y, lax.rem(z + d, NZ) * NJ + j) for d in range(1, NZ)]
     turns = [(dy, dj) for dj in range(NJ) for dy in range(SITES) if dy or dj]
     plane_peers = [(lax.rem(y + dy, SITES), z * NJ + lax.rem(j + dj, NJ)) for dy, dj in turns]
-    greet(plane_peers + z_peers)
+    barrier = pltpu.get_barrier_semaphore()
+    for peer in plane_peers + z_peers:
+        pl.semaphore_signal(barrier, inc=1, device_id=peer, device_id_type=MESH)
+    slip_load.wait()
     for v in range(4):
         for zz in range(2):
             for jj in range(NJ):
                 at = (zz * NJ + jj) * PTS
                 for k in range(3):
                     mine[v, jj, zz, k] = slip_ref[k, v : v + 1, at : at + PTS]
+    pl.semaphore_wait(barrier, len(plane_peers) + len(z_peers))
     copies = []
     for d, peer in enumerate(plane_peers):
         copy = remote(
@@ -110,6 +127,7 @@
         copies.append(copy)
     plane[j, pl.ds(2 * y, 2)] = mine[y, j]
 
+    mech_load.wait()
     turned = jnp.transpose(jnp.concatenate([mech_ref[...], jnp.zeros((2, PTS), F32)], axis=0))
     for k in range(6):
         mech_wide[k] = jnp.broadcast_to(turned[:, k : k + 1], (PTS, PTS))
@@ -121,10 +139,15 @@
                 total = mech_wide[0] * sgt[c, 0, part, :, pl.ds(at, PTS)].astype(F32)
                 for k in range(1, 6):
                     total = total + mech_wide[k] * sgt[c, k, part, :, pl.ds(at, PTS)].astype(F32)
-                turned = jnp.transpose(total)
-                rows = at * 4 + 2 * c
-                weights_ref[part, pl.ds(rows, PTS, stride=4), :] = turned
-                weights_ref[1 - part, pl.ds(rows + 1, PTS, stride=4), :] = turned if part else -turned
+                turning[part] = jnp.transpose(total)
+                for parity in range(2):
+                    picked = turning[part, pl.ds(parity, PTS // 2, stride=2), :]
+                    for half in range(2):
+                        group = step * 4 + half * 2 + parity
+                        value = picked[half * 32 : half * 32 + 32]
+                        same, other = slice(part * PTS, part * PTS + PTS), slice((1 - part) * PTS, (2 - part) * PTS)
+                        weights[group, 64 * c : 64 * c + 32, same] = value.astype(BF16)
+                        weights[group, 64 * c + 32 : 64 * c + 64, other] = (value if part else -value).astype(BF16)
             return carry
 
         lax.fori_loop(0, FREQ // PTS, tile, 0)
@@ -198,63 +221,6 @@
         return carry
 
     lax.fori_loop(0, OWNERS, select, 0)
-
-
-def fields_and_weights(sgt, mechanism, slip, start, count, order):
-    dma = pltpu.SemaphoreType.DMA
-    smem = pl.BlockSpec(memory_space=pltpu.SMEM)
-    vmem = pl.BlockSpec(memory_space=pltpu.VMEM)
-    return pl.pallas_call(
-        fields_kernel,
-        out_shape=(
-            jax.ShapeDtypeStruct((3, OWNERS, PTS), F32),
-            jax.ShapeDtypeStruct((2, FREQ * 4, PTS), F32),
-            jax.ShapeDtypeStruct((2, 4 * NZ, 128), jnp.int32),
-        ),
-        in_specs=[smem, smem, smem, vmem, vmem, pl.BlockSpec(memory_space=pl.ANY)],
-        out_specs=(vmem, vmem, vmem),
-        scratch_shapes=[
-            pltpu.VMEM((4, NJ, 2, 3, 1, PTS), F32),
-            pltpu.VMEM((NJ, NZ, 3, 1, PTS), F32),
-            pltpu.VMEM((4, NZ, NJ, 3, 1, PTS), F32),
-            pltpu.SMEM((OWNERS,), jnp.int32),
-            pltpu.SMEM((OWNERS,), jnp.int32),
-            pltpu.VMEM((6, PTS, PTS), F32),
-            pltpu.VMEM((2, 6, 2, PTS, FREQ), BF16),
-            dma((31,)), dma((31,)), dma((7,)), dma((7,)), dma((8, 3)), dma((8, 3)), dma((2,)),
-        ],
-        compiler_params=pltpu.CompilerParams(
-            collective_id=0, has_side_effects=True, vmem_limit_bytes=40 * 2**20
-        ),
-        name="fields_and_weights",
-    )(start, count, order, jnp.transpose(slip, (1, 0, 2)), mechanism, sgt)
-
-
-def circle(turns):
-    half = (turns - jnp.floor(turns + 0.5)) * jnp.float32(np.pi)
-    sq = half * half
-    sine = jnp.float32(1.0 / 6227020800)
-    for sign, power in ((-1, 39916800), (1, 362880), (-1, 5040), (1, 120), (-1, 6)):
-        sine = sine * sq + jnp.float32(sign / power)
-    sine = half + half * sq * sine
-    cosine = jnp.float32(-1.0 / 87178291200)
-    for sign, power in ((1, 479001600), (-1, 3628800), (1, 40320), (-1, 720), (1, 24), (-1, 2)):
-        cosine = cosine * sq + jnp.float32(sign / power)
-    cosine = cosine * sq + 1.0
-    return 1.0 - 2.0 * sine * sine, 2.0 * sine * cosine
-
-
-def peaks_kernel(
-    inverse_ref, fields_ref, weights_ref, limits_ref, response_ref, table_ref, out_ref,
-    state, source_cos, source_sin, sums, parts, arrived, summed, landed, left, extra, total_series, best,
-    send_a, recv_a, send_b, recv_b,
-):
-    y, b, z, j = place()
-    j_peers = [(y, z * NJ + lax.rem(j + d, NJ)) for d in range(1, NJ)]
-    z_peers = [(y, lax.rem(z + d, NZ) * NJ + j) for d in range(1, NZ)]
-    barrier = pltpu.get_barrier_semaphore()
-    for peer in j_peers + z_peers:
-        pl.semaphore_signal(barrier, inc=1, device_id=peer, device_id_type=MESH)
 
     amp = fields_ref[0]
     turns = fields_ref[1] * jnp.float32(TURNS)
@@ -273,50 +239,62 @@
     state[7] = jump_s
     state[9] = rise * rise
 
-    def run(turn, carry):
-        base = turn * (2 * STEPS)
+    half_lane = lax.broadcasted_iota(jnp.int32, (OWNERS, 128), 1) & 31
+
+    def sources_of(turn, parity):
+        base = turn * (2 * STEPS) + parity
         for pair in range(OWNERS // 16):
             rows = slice(pair * 16, pair * 16 + 16)
             double = state[8, rows]
             rise_sq = state[9, rows]
-            for parity in range(2):
-                cos_now, sin_now = state[2 * parity, rows], state[2 * parity + 1, rows]
-                step_c, step_s = state[4, rows], state[5, rows]
-                jump_c, jump_s = state[6, rows], state[7, rows]
-                state[2 * parity, rows] = cos_now * jump_c - sin_now * jump_s
-                state[2 * parity + 1, rows] = sin_now * jump_c + cos_now * jump_s
-                cos_next = cos_now * step_c - sin_now * step_s
-                sin_next = sin_now * step_c + cos_now * step_s
-                at = parity * OWNERS + pair * 16
-                for i in range(STEPS):
-                    scale = lax.rsqrt(rise_sq + inverse_ref[base + (2 * i + parity)])
-                    source_cos[i, at : at + 16, :] = (cos_now * scale).astype(BF16)
-                    source_sin[i, at : at + 16, :] = (sin_now * scale).astype(BF16)
-                    if i < STEPS - 1:
-                        cos_now, cos_next = cos_next, double * cos_next - cos_now
-                        sin_now, sin_next = sin_next, double * sin_next - sin_now
-        local = lax.rem(turn, 128 // STEPS) * STEPS
-        for i in range(0, STEPS, 2):
-            first = pl.multiple_of((turn * STEPS + i) * 8, 16)
-            lhs = jnp.concatenate([weights_ref[0, pl.ds(first, 16)], weights_ref[1, pl.ds(first, 16)]], axis=1).astype(BF16)
-            rhs = jnp.concatenate(
-                [source_cos[i : i + 2].reshape(2 * PTS, PTS), source_sin[i : i + 2].reshape(2 * PTS, PTS)], axis=1
+            cos_now, sin_now = state[2 * parity, rows], state[2 * parity + 1, rows]
+            step_c, step_s = state[4, rows], state[5, rows]
+            jump_c, jump_s = state[6, rows], state[7, rows]
+            state[2 * parity, rows] = cos_now * jump_c - sin_now * jump_s
+            state[2 * parity + 1, rows] = sin_now * jump_c + cos_now * jump_s
+            cos_next = cos_now * step_c - sin_now * step_s
+            sin_next = sin_now * step_c + cos_now * step_s
+            for i in range(STEPS):
+                scale = lax.rsqrt(rise_sq + inverse_ref[base + 2 * i])
+                source_cos[parity, i, rows, :] = (cos_now * scale).astype(BF16)
+                source_sin[parity, i, rows, :] = (sin_now * scale).astype(BF16)
+                if i < STEPS - 1:
+                    cos_now, cos_next = cos_next, double * cos_next - cos_now
+                    sin_now, sin_next = sin_next, double * sin_next - sin_now
+
+    def sums_of(h, local, turn, parity):
+        rhs = weights[turn * 2 + parity]
+        total = jnp.zeros((OWNERS, 128), F32)
+        for i0 in range(0, STEPS, 16):
+            lhs = jnp.concatenate(
+                [ref[parity, i0 : i0 + 16].reshape(16 * OWNERS, PTS) for ref in (source_cos, source_sin)], axis=1
             )
             product = lax.dot_general(lhs, rhs, (((1,), (1,)), ((), ())), preferred_element_type=F32)
-            sums[pl.ds(local + i, 8, stride=128), :] = product[0:8, 0:128]
-            sums[pl.ds(local + i + 1, 8, stride=128), :] = product[8:16, 128:256]
-        return carry
+            for i in range(16):
+                total = jnp.where(half_lane == i0 + i, product[i * OWNERS : (i + 1) * OWNERS], total)
+        parts[h, parity * 4 + local] = total
+
+    def spectra_of(h):
+        def run(local, carry):
+            turn = h * 4 + local
+            sums_of(h, local - 1, turn - 1, 1)
+            sources_of(turn, 0)
+            sums_of(h, local, turn, 0)
+            sources_of(turn, 1)
+            return carry
+
+        sources_of(h * 4, 0)
+        sums_of(h, 0, h * 4, 0)
+        sources_of(h * 4, 1)
+        lax.fori_loop(1, 4, run, 0)
+        sums_of(h, 3, h * 4 + 3, 1)
 
     def send_parts(h):
-        for row in range(8):
-            turned = jnp.transpose(sums[row * 128 : (row + 1) * 128, :])
-            parity = row // 4
-            parts[h, row] = turned[parity * OWNERS : (parity + 1) * OWNERS]
         copies = []
         for d, peer in enumerate(j_peers):
             rows = pl.multiple_of(lax.rem(j + d + 1, NJ) * NZ, 8)
             copy = remote(
-                parts.at[h, :, pl.ds(rows, NZ), :], arrived.at[h, j], send_a.at[h, d], recv_a.at[h, d], peer
+                parts.at[h, :, pl.ds(rows, NZ), :], arrived.at[h, j], send_d.at[h, d], recv_d.at[h, d], peer
             )
             copy.start()
             copies.append(copy)
@@ -340,14 +318,13 @@
         for d, peer in enumerate(z_peers):
             rows = pl.multiple_of(lax.rem(z + d + 1, NZ) * 32, 32)
             copy = remote(
-                summed.at[h, pl.ds(rows, 32), :], landed.at[h, z], send_b.at[h, d], recv_b.at[h, d], peer
+                summed.at[h, pl.ds(rows, 32), :], landed.at[h, z], send_e.at[h, d], recv_e.at[h, d], peer
             )
             copy.start()
             copies.append(copy)
         landed[h, z] = summed[h, pl.ds(pl.multiple_of(z * 32, 32), 32), :]
         return copies
 
-    lane = lax.broadcasted_iota(jnp.int32, (1, 128), 1)
     sign = jnp.where(lax.rem(lane, 2) == 0, 1.0, -1.0).astype(F32)
 
     def respond(h, copies):
@@ -356,14 +333,21 @@
         total = landed[h, 0]
         for src in range(1, NZ):
             total = total + landed[h, src]
+        moved = [total] + [pltpu.roll(total, 32 * d, 1) for d in range(1, 4)]
+        segment = lax.shift_right_logical(lane, 5)
+
+        def lined(first, k):
+            rows = [moved[(g - k) % 4][first + g : first + g + 1] for g in range(4)]
+            return jnp.where(segment < 2, jnp.where(segment < 1, rows[0], rows[1]), jnp.where(segment < 3, rows[2], rows[3]))
+
         cols = slice(h * 128, h * 128 + 128)
         for parity in range(2):
             stiff = response_ref[parity, 0, :, cols]
             friction = response_ref[parity, 1, :, cols]
             for slot in range(4):
                 for c in range(2):
-                    row = slot * 8 + parity * 4 + 2 * c
-                    real, imag = total[row : row + 1], total[row + 1 : row + 2]
+                    first = slot * 8 + parity * 4
+                    real, imag = lined(first, 2 * c), lined(first, 2 * c + 1)
                     rows = slice((slot * 2 + c) * PAD_PERIODS, (slot * 2 + c + 1) * PAD_PERIODS)
                     for part, value in enumerate(
                         (real * stiff + imag * friction, imag * stiff - real * friction)
@@ -421,17 +405,17 @@
 
         lax.fori_loop(0, 4, tile, 0)
 
-    turns_each = 128 // STEPS
     first_hop, second_hop = {}, {}
     for h in range(CHUNKS):
-        lax.fori_loop(h * turns_each, (h + 1) * turns_each, run, 0)
-        if h == 0:
-            pl.semaphore_wait(barrier, len(j_peers) + len(z_peers))
+        spectra_of(h)
         first_hop[h] = send_parts(h)
         if h >= 1:
             second_hop[h - 1] = send_sums(h - 1, first_hop[h - 1])
+        if h == 2:
+            response_load.wait()
         if h >= 2:
             respond(h - 2, second_hop[h - 2])
+    table_load.wait()
     for h in range(2):
         add_series(h)
     second_hop[3] = send_sums(3, first_hop[3])
@@ -451,19 +435,34 @@
         out_ref[0, slot : slot + 1, :] = row[:, : 2 * PERIODS]
 
 
-def owner_peaks(inverse, fields, weights, limits, response, tables):
+def program(start, count, order, inverse, slip, mechanism, sgt, response, tables):
     dma = pltpu.SemaphoreType.DMA
-    vmem = pl.BlockSpec(memory_space=pltpu.VMEM)
+    smem = pl.BlockSpec(memory_space=pltpu.SMEM)
+    hbm = pl.BlockSpec(memory_space=pl.ANY)
     return pl.pallas_call(
-        peaks_kernel,
+        kernel,
         out_shape=jax.ShapeDtypeStruct((1, 4, 2 * PERIODS), F32),
-        in_specs=[pl.BlockSpec(memory_space=pltpu.SMEM)] + [vmem] * 5,
-        out_specs=vmem,
+        in_specs=[smem] * 4 + [hbm] * 5,
+        out_specs=pl.BlockSpec(memory_space=pltpu.VMEM),
         scratch_shapes=[
+            pltpu.VMEM((3, 4, 2 * NJ * PTS), F32),
+            pltpu.VMEM((6, PTS), F32),
+            pltpu.VMEM((2, 6, 2, PTS, FREQ), BF16),
+            pltpu.VMEM(response.shape, F32),
+            pltpu.VMEM(tables.shape, BF16),
+            pltpu.VMEM((4, NJ, 2, 3, 1, PTS), F32),
+            pltpu.VMEM((NJ, NZ, 3, 1, PTS), F32),
+            pltpu.VMEM((4, NZ, NJ, 3, 1, PTS), F32),
+            pltpu.SMEM((OWNERS,), jnp.int32),
+            pltpu.SMEM((OWNERS,), jnp.int32),
+            pltpu.VMEM((6, PTS, PTS), F32),
+            pltpu.VMEM((2, PTS, PTS), F32),
+            pltpu.VMEM((FREQ // 32, PTS, 2 * PTS), BF16),
+            pltpu.VMEM((2, 4 * NZ, 128), jnp.int32),
+            pltpu.VMEM((3, OWNERS, PTS), F32),
             pltpu.VMEM((10, OWNERS, PTS), F32),
-            pltpu.VMEM((STEPS, 2 * OWNERS, PTS), BF16),
-            pltpu.VMEM((STEPS, 2 * OWNERS, PTS), BF16),
-            pltpu.VMEM((8 * 128, 128), F32),
+            pltpu.VMEM((2, STEPS, OWNERS, PTS), BF16),
+            pltpu.VMEM((2, STEPS, OWNERS, PTS), BF16),
             pltpu.VMEM((CHUNKS, 8, OWNERS, 128), F32),
             pltpu.VMEM((CHUNKS, NJ, 8, NZ, 128), F32),
             pltpu.VMEM((CHUNKS, NZ * 32, 128), F32),
@@ -472,24 +471,23 @@
             pltpu.VMEM((ROWS, 128), F32),
             pltpu.VMEM((2, 2, ROWS, HALF), F32),
             pltpu.VMEM((ROWS, 128), F32),
+            dma((6,)), dma((31,)), dma((31,)), dma((7,)), dma((7,)), dma((8, 3)), dma((8, 3)),
             dma((CHUNKS, 7)), dma((CHUNKS, 7)), dma((CHUNKS, 7)), dma((CHUNKS, 7)),
         ],
         compiler_params=pltpu.CompilerParams(
-            collective_id=1, has_side_effects=True, vmem_limit_bytes=48 * 2**20
+            collective_id=0, has_side_effects=True, vmem_limit_bytes=60 * 2**20
         ),
-        name="owner_peaks",
-    )(inverse, fields, weights, limits, response, tables)
+        name="spectral_accelerations",
+    )(start, count, order, inverse, jnp.transpose(slip, (1, 0, 2)), mechanism, sgt, response, tables)
 
 
 def solution(mesh):
     response, tables, inverse = constant_tables()
 
     def per_device(sgt, mechanism, slip_fields, rupture_start, point_count, owner_order):
-        fields, weights, limits = fields_and_weights(
-            sgt, mechanism, slip_fields, rupture_start, point_count, owner_order
-        )
-        return owner_peaks(
-            jnp.asarray(inverse), fields, weights, limits, jnp.asarray(response), jnp.asarray(tables)
+        return program(
+            rupture_start, point_count, owner_order, jnp.asarray(inverse), slip_fields, mechanism, sgt,
+            jnp.asarray(response), jnp.asarray(tables),
         )
 
     return jax.shard_map(

time: 72.6 us -> 64.2 us (0.88)
  local copies, waits for them, and re-layouts: 6.99 us -> 1.26 us
  Pallas kernels: 65.3 us -> 62.8 us
    unnamed x17 -> x1, local copies, waits for them, and re-layouts: 6.99 us -> 1.26 us
    pallas_call x2 -> x1, Pallas kernels: 65.3 us -> 62.8 us  [program(): pl.pallas_call(kernel, out_shape=jax.ShapeDtypeStruct((1, 4, 2 * PERIODS)...]
where the time goes in v3:
time: 64.2 us; the launch traced here: 64.1 us
  Pallas kernels  62.8 us (98%)
  local copies, waits for them, and re-layouts  1.26 us (2%)
    pallas_call x1, Pallas kernels, program(): pl.pallas_call(kernel, out_shape=jax.ShapeDtypeStruct((1, 4, 2 * PERIODS)...  62.8 us

profile of v3, /device:TPU:1, one launch (start us, length us, event | category | flops | bytes accessed | tf_op | source)
XLA Modules:
  0.0 64.1 jit_solution(9948913506638575902)
XLA Ops:
  0.0 62.8 %spectral_accelerations.1 = f32[1,4,88]{2,1,0:T(4,128)} custom-call(s32[256]{0:T(256)} %start_ref.1, s32[256]{0:T(256)} %count_ref.1, s32[256]{0:T(256)} %order_ref.1, f32[1024]{0:T(1024)} %constant.6.clone.inverse_ref, f32[3,4,2048]{2,1,0:T(4,128)} %bitcast.1, f32[6,128]{1,0:T(8,128)} %mech_hbm.1, bf16[1,2,6,2,128,1024]{5,4,3,2,1,0:T(8,128)(2,1)} %sgt_hbm.1, ...), custom_call_target="tpu_custom_call" | custom-call | tf_op jit(solution)/shard_map/spectral_accelerations/pallas_call | solution.py:442
  62.8 1.3 %copy.11 = f32[1,4,88]{2,1,0:T(4,128)} copy(f32[1,4,88]{2,1,0:T(4,128)} %spectral_accelerations.1) | data formatting | bytes 2816

commit v4 on v3

--- a/solution.py
+++ b/solution.py
@@ -58,7 +58,8 @@
         if parity == 1:
             sine[:, 0] = np.where(np.arange(HALF) % 2 == 0, 1.0, -1.0)
         tables[parity, 1, 0], tables[parity, 1, 1] = split_table(sine)
-    return response, tables, (1.0 / number**2).astype(np.float32)
+    inverse = np.broadcast_to((1.0 / number**2).astype(np.float32)[:, None, None], (FREQ, 8, 128))
+    return response, tables, np.ascontiguousarray(inverse)
 
 
 def place():
@@ -88,8 +89,8 @@
 
 
 def kernel(
-    start_ref, count_ref, order_ref, inverse_ref, slip_hbm, mech_hbm, sgt_hbm, response_hbm, table_hbm, out_ref,
-    slip_ref, mech_ref, sgt, response_ref, table_ref,
+    start_hbm, count_hbm, order_hbm, inverse_hbm, slip_hbm, mech_hbm, sgt_hbm, response_hbm, table_hbm, out_ref,
+    start_ref, count_ref, order_ref, inverse_ref, slip_ref, mech_ref, sgt, response_ref, table_ref,
     mine, plane, block, chosen, points, mech_wide, turning, weights, limits_ref, fields_ref,
     state, source_cos, source_sin, parts, arrived, summed, landed, left, extra, total_series, best,
     load_sem, send_a, recv_a, send_b, recv_b, send_c, recv_c, send_d, recv_d, send_e, recv_e,
@@ -100,7 +101,14 @@
     loads = [pltpu.make_async_copy(sgt_hbm.at[0, c], sgt.at[c], load_sem.at[c]) for c in range(2)]
     response_load = pltpu.make_async_copy(response_hbm, response_ref, load_sem.at[4])
     table_load = pltpu.make_async_copy(table_hbm, table_ref, load_sem.at[5])
-    for load in (slip_load, mech_load, *loads, response_load, table_load):
+    index_loads = [
+        pltpu.make_async_copy(src, dst, load_sem.at[6 + k])
+        for k, (src, dst) in enumerate(
+            ((start_hbm, start_ref), (count_hbm, count_ref), (order_hbm, order_ref))
+        )
+    ]
+    inverse_load = pltpu.make_async_copy(inverse_hbm, inverse_ref, load_sem.at[9])
+    for load in (slip_load, mech_load, *loads, *index_loads, inverse_load, response_load, table_load):
         load.start()
     y_peers = [(lax.rem(y + d, SITES), b) for d in range(1, SITES)]
     j_peers = [(y, z * NJ + lax.rem(j + d, NJ)) for d in range(1, NJ)]
@@ -173,6 +181,9 @@
 
     forward(0, z)
 
+    for load in index_loads:
+        load.wait()
+
     def choose(row, carry):
         owner = lax.rem(row, NZ) * NJ + lax.div(row, NZ)
         best = jnp.int32(0)
@@ -239,7 +250,7 @@
     state[7] = jump_s
     state[9] = rise * rise
 
-    half_lane = lax.broadcasted_iota(jnp.int32, (OWNERS, 128), 1) & 31
+    half_lane = lax.broadcasted_iota(jnp.int32, (8, 128), 1) & 31
 
     def sources_of(turn, parity):
         base = turn * (2 * STEPS) + parity
@@ -255,74 +266,79 @@
             cos_next = cos_now * step_c - sin_now * step_s
             sin_next = sin_now * step_c + cos_now * step_s
             for i in range(STEPS):
-                scale = lax.rsqrt(rise_sq + inverse_ref[base + 2 * i])
+                inverse = inverse_ref[base + 2 * i]
+                scale = lax.rsqrt(rise_sq + jnp.concatenate([inverse, inverse], axis=0))
                 source_cos[parity, i, rows, :] = (cos_now * scale).astype(BF16)
                 source_sin[parity, i, rows, :] = (sin_now * scale).astype(BF16)
                 if i < STEPS - 1:
                     cos_now, cos_next = cos_next, double * cos_next - cos_now
                     sin_now, sin_next = sin_next, double * sin_next - sin_now
 
-    def sums_of(h, local, turn, parity):
+    def sums_of(turn, parity):
         rhs = weights[turn * 2 + parity]
-        total = jnp.zeros((OWNERS, 128), F32)
+        total = None
         for i0 in range(0, STEPS, 16):
             lhs = jnp.concatenate(
                 [ref[parity, i0 : i0 + 16].reshape(16 * OWNERS, PTS) for ref in (source_cos, source_sin)], axis=1
             )
             product = lax.dot_general(lhs, rhs, (((1,), (1,)), ((), ())), preferred_element_type=F32)
             for i in range(16):
-                total = jnp.where(half_lane == i0 + i, product[i * OWNERS : (i + 1) * OWNERS], total)
-        parts[h, parity * 4 + local] = total
-
-    def spectra_of(h):
-        def run(local, carry):
-            turn = h * 4 + local
-            sums_of(h, local - 1, turn - 1, 1)
-            sources_of(turn, 0)
-            sums_of(h, local, turn, 0)
-            sources_of(turn, 1)
-            return carry
-
-        sources_of(h * 4, 0)
-        sums_of(h, 0, h * 4, 0)
-        sources_of(h * 4, 1)
-        lax.fori_loop(1, 4, run, 0)
-        sums_of(h, 3, h * 4 + 3, 1)
-
-    def send_parts(h):
+                rows = [product[i * OWNERS + k * 8 : i * OWNERS + k * 8 + 8] for k in range(OWNERS // 8)]
+                if total is None:
+                    total = rows
+                else:
+                    own = half_lane == i0 + i
+                    total = [jnp.where(own, new, old) for new, old in zip(rows, total)]
+        for k in range(OWNERS // 8):
+            parts[turn * 2 + parity, k * 8 : k * 8 + 8] = total[k]
+
+    def turn_of(turn, carry):
+        sums_of(turn - 1, 1)
+        sources_of(turn, 0)
+        sums_of(turn, 0)
+        sources_of(turn, 1)
+        return carry
+
+    pieces = [(0, 8), (8, 8), (16, 4), (20, 4), (24, 4), (28, 4)]
+
+    def send_parts(index):
+        at, size = pieces[index]
+        groups = pl.ds(at, size)
         copies = []
         for d, peer in enumerate(j_peers):
             rows = pl.multiple_of(lax.rem(j + d + 1, NJ) * NZ, 8)
             copy = remote(
-                parts.at[h, :, pl.ds(rows, NZ), :], arrived.at[h, j], send_d.at[h, d], recv_d.at[h, d], peer
+                parts.at[groups, pl.ds(rows, NZ), :], arrived.at[j, groups], send_d.at[index, d], recv_d.at[index, d], peer
             )
             copy.start()
             copies.append(copy)
-        arrived[h, j] = parts[h, :, pl.ds(pl.multiple_of(j * NZ, 8), NZ), :]
+        arrived[j, groups] = parts[groups, pl.ds(pl.multiple_of(j * NZ, 8), NZ), :]
         return copies
 
-    def send_sums(h, copies):
+    def send_sums(index, copies):
+        at, size = pieces[index]
         for copy in copies:
             copy.wait()
         for slot in range(4):
             first = limits_ref[0, slot * NZ : slot * NZ + NZ]
             last = limits_ref[1, slot * NZ : slot * NZ + NZ]
-            total = jnp.zeros((8, NZ, 128), F32)
+            total = jnp.zeros((size, NZ, 128), F32)
             for src in range(NJ):
-                at = z * NJ + src
-                live = (first <= at) & (at < last)
-                total = total + jnp.where(live[None], arrived[h, src], 0.0)
-            for row in range(8):
-                summed[h, pl.ds(slot * 8 + row, NZ, stride=32), :] = total[row]
+                block_id = z * NJ + src
+                live = (first <= block_id) & (block_id < last)
+                total = total + jnp.where(live[None], arrived[src, at : at + size], 0.0)
+            for row in range(size):
+                summed[pl.ds(at * 32 + slot * size + row, NZ, stride=4 * size), :] = total[row]
         copies = []
         for d, peer in enumerate(z_peers):
-            rows = pl.multiple_of(lax.rem(z + d + 1, NZ) * 32, 32)
+            rows = pl.multiple_of(at * 32 + lax.rem(z + d + 1, NZ) * (4 * size), 8)
             copy = remote(
-                summed.at[h, pl.ds(rows, 32), :], landed.at[h, z], send_e.at[h, d], recv_e.at[h, d], peer
+                summed.at[pl.ds(rows, 4 * size), :], landed.at[z, pl.ds(4 * at, 4 * size)],
+                send_e.at[index, d], recv_e.at[index, d], peer,
             )
             copy.start()
             copies.append(copy)
-        landed[h, z] = summed[h, pl.ds(pl.multiple_of(z * 32, 32), 32), :]
+        landed[z, pl.ds(4 * at, 4 * size)] = summed[pl.ds(pl.multiple_of(at * 32 + z * (4 * size), 8), 4 * size), :]
         return copies
 
     sign = jnp.where(lax.rem(lane, 2) == 0, 1.0, -1.0).astype(F32)
@@ -330,14 +346,19 @@
     def respond(h, copies):
         for copy in copies:
             copy.wait()
-        total = landed[h, 0]
+        total = landed[0, h * 32 : h * 32 + 32]
         for src in range(1, NZ):
-            total = total + landed[h, src]
+            total = total + landed[src, h * 32 : h * 32 + 32]
+        size = 8 if h < 2 else 4
         moved = [total] + [pltpu.roll(total, 32 * d, 1) for d in range(1, 4)]
         segment = lax.shift_right_logical(lane, 5)
 
-        def lined(first, k):
-            rows = [moved[(g - k) % 4][first + g : first + g + 1] for g in range(4)]
+        def lined(slot, parity, k):
+            rows = []
+            for g in range(4):
+                group = g * 2 + parity
+                row = group // size * 4 * size + slot * size + group % size
+                rows.append(moved[(g - k) % 4][row : row + 1])
             return jnp.where(segment < 2, jnp.where(segment < 1, rows[0], rows[1]), jnp.where(segment < 3, rows[2], rows[3]))
 
         cols = slice(h * 128, h * 128 + 128)
@@ -346,8 +367,7 @@
             friction = response_ref[parity, 1, :, cols]
             for slot in range(4):
                 for c in range(2):
-                    first = slot * 8 + parity * 4
-                    real, imag = lined(first, 2 * c), lined(first, 2 * c + 1)
+                    real, imag = lined(slot, parity, 2 * c), lined(slot, parity, 2 * c + 1)
                     rows = slice((slot * 2 + c) * PAD_PERIODS, (slot * 2 + c + 1) * PAD_PERIODS)
                     for part, value in enumerate(
                         (real * stiff + imag * friction, imag * stiff - real * friction)
@@ -406,45 +426,70 @@
         lax.fori_loop(0, 4, tile, 0)
 
     first_hop, second_hop = {}, {}
-    for h in range(CHUNKS):
-        spectra_of(h)
-        first_hop[h] = send_parts(h)
-        if h >= 1:
-            second_hop[h - 1] = send_sums(h - 1, first_hop[h - 1])
-        if h == 2:
-            response_load.wait()
-        if h >= 2:
-            respond(h - 2, second_hop[h - 2])
+    inverse_load.wait()
+    sources_of(0, 0)
+    sums_of(0, 0)
+    sources_of(0, 1)
+    lax.fori_loop(1, 5, turn_of, 0)
+    first_hop[0] = send_parts(0)
+    lax.fori_loop(5, 9, turn_of, 0)
+    first_hop[1] = send_parts(1)
+    second_hop[0] = send_sums(0, first_hop[0])
+    lax.fori_loop(9, 11, turn_of, 0)
+    first_hop[2] = send_parts(2)
+    lax.fori_loop(11, 13, turn_of, 0)
+    first_hop[3] = send_parts(3)
+    second_hop[1] = send_sums(1, first_hop[1])
+    response_load.wait()
+    respond(0, second_hop[0])
+    lax.fori_loop(13, 15, turn_of, 0)
+    first_hop[4] = send_parts(4)
+    second_hop[2] = send_sums(2, first_hop[2])
+    lax.fori_loop(15, 16, turn_of, 0)
+    sums_of(15, 1)
+    first_hop[5] = send_parts(5)
+    second_hop[3] = send_sums(3, first_hop[3])
+    second_hop[4] = send_sums(4, first_hop[4])
+    respond(1, second_hop[1])
     table_load.wait()
-    for h in range(2):
-        add_series(h)
-    second_hop[3] = send_sums(3, first_hop[3])
-    respond(2, second_hop[2])
+    add_series(0)
+    second_hop[5] = send_sums(5, first_hop[5])
+    add_series(1)
+    respond(2, second_hop[2] + second_hop[3])
     add_series(2)
-    respond(3, second_hop[3])
+    respond(3, second_hop[4] + second_hop[5])
     last_series(3)
 
+    turned = [jnp.transpose(best[at : at + 128]) for at in range(0, ROWS, 128)]
+    peaks = [jnp.max(value, axis=0, keepdims=True) for value in turned]
+
+    def placed(first, lanes):
+        at, offset = divmod(first, 128)
+        shift = (lanes - offset) % 128
+        moved = [pltpu.roll(value, shift, 1) if shift else value for value in peaks[at : at + 2]]
+        if offset + PERIODS <= 128:
+            return moved[0]
+        return jnp.where(lane < lanes + 128 - offset, moved[0], moved[1])
+
     for slot in range(4):
-        pieces = []
-        for c in range(2):
-            at = (slot * 2 + c) * PAD_PERIODS
-            turned = jnp.transpose(jnp.concatenate([best[at : at + PAD_PERIODS], jnp.zeros((128 - PAD_PERIODS, 128), F32)], axis=0))
-            pieces.append(jnp.max(turned, axis=0, keepdims=True))
-        moved = pltpu.roll(pieces[1], PERIODS, 1)
-        row = jnp.where(lane < PERIODS, pieces[0], moved)
+        first = slot * 2 * PAD_PERIODS
+        row = jnp.where(lane < PERIODS, placed(first, 0), placed(first + PAD_PERIODS, PERIODS))
         out_ref[0, slot : slot + 1, :] = row[:, : 2 * PERIODS]
 
 
 def program(start, count, order, inverse, slip, mechanism, sgt, response, tables):
     dma = pltpu.SemaphoreType.DMA
-    smem = pl.BlockSpec(memory_space=pltpu.SMEM)
     hbm = pl.BlockSpec(memory_space=pl.ANY)
     return pl.pallas_call(
         kernel,
         out_shape=jax.ShapeDtypeStruct((1, 4, 2 * PERIODS), F32),
-        in_specs=[smem] * 4 + [hbm] * 5,
+        in_specs=[hbm] * 9,
         out_specs=pl.BlockSpec(memory_space=pltpu.VMEM),
         scratch_shapes=[
+            pltpu.SMEM(start.shape, jnp.int32),
+            pltpu.SMEM(count.shape, jnp.int32),
+            pltpu.SMEM(order.shape, jnp.int32),
+            pltpu.VMEM(inverse.shape, F32),
             pltpu.VMEM((3, 4, 2 * NJ * PTS), F32),
             pltpu.VMEM((6, PTS), F32),
             pltpu.VMEM((2, 6, 2, PTS, FREQ), BF16),
@@ -463,16 +508,16 @@
             pltpu.VMEM((10, OWNERS, PTS), F32),
             pltpu.VMEM((2, STEPS, OWNERS, PTS), BF16),
             pltpu.VMEM((2, STEPS, OWNERS, PTS), BF16),
-            pltpu.VMEM((CHUNKS, 8, OWNERS, 128), F32),
-            pltpu.VMEM((CHUNKS, NJ, 8, NZ, 128), F32),
-            pltpu.VMEM((CHUNKS, NZ * 32, 128), F32),
-            pltpu.VMEM((CHUNKS, NZ, 32, 128), F32),
+            pltpu.VMEM((FREQ // 32, OWNERS, 128), F32),
+            pltpu.VMEM((NJ, FREQ // 32, NZ, 128), F32),
+            pltpu.VMEM((FREQ // 32 * 4 * NZ, 128), F32),
+            pltpu.VMEM((NZ, FREQ // 32 * 4, 128), F32),
             pltpu.VMEM((CHUNKS, 2, 2, ROWS, 256), BF16),
             pltpu.VMEM((ROWS, 128), F32),
             pltpu.VMEM((2, 2, ROWS, HALF), F32),
             pltpu.VMEM((ROWS, 128), F32),
-            dma((6,)), dma((31,)), dma((31,)), dma((7,)), dma((7,)), dma((8, 3)), dma((8, 3)),
-            dma((CHUNKS, 7)), dma((CHUNKS, 7)), dma((CHUNKS, 7)), dma((CHUNKS, 7)),
+            dma((10,)), dma((31,)), dma((31,)), dma((7,)), dma((7,)), dma((8, 3)), dma((8, 3)),
+            dma((6, 7)), dma((6, 7)), dma((6, 7)), dma((6, 7)),
         ],
         compiler_params=pltpu.CompilerParams(
             collective_id=0, has_side_effects=True, vmem_limit_bytes=60 * 2**20

time: 64.2 us -> 62.8 us (0.978)
  Pallas kernels: 62.8 us -> 61.5 us
    pallas_call x1, Pallas kernels: 62.8 us -> 61.5 us  [program(): pl.pallas_call(kernel, out_shape=jax.ShapeDtypeStruct((1, 4, 2 * PERIODS)...]
where the time goes in v4:
time: 62.8 us; the launch traced here: 62.7 us
  Pallas kernels  61.5 us (98%)
  local copies, waits for them, and re-layouts  1.26 us (2%)
    pallas_call x1, Pallas kernels, program(): pl.pallas_call(kernel, out_shape=jax.ShapeDtypeStruct((1, 4, 2 * PERIODS)...  61.5 us
    unnamed x1, local copies, waits for them, and re-layouts  1.26 us

profile of v4, /device:TPU:1, one launch (start us, length us, event | category | flops | bytes accessed | tf_op | source)
XLA Modules:
  0.0 62.7 jit_solution(2597437406138731130)
XLA Ops:
  0.0 61.5 %spectral_accelerations.1 = f32[1,4,88]{2,1,0:T(4,128)} custom-call(s32[256]{0:T(256)} %start_hbm.1, s32[256]{0:T(256)} %count_hbm.1, s32[256]{0:T(256)} %order_hbm.1, f32[1024,8,128]{2,1,0:T(8,128)} %constant.6.clone.inverse_hbm, f32[3,4,2048]{2,1,0:T(4,128)} %bitcast.1, f32[6,128]{1,0:T(8,128)} %mech_hbm.1, bf16[1,2,6,2,128,1024]{5,4,3,2,1,0:T(8,128)(2,1)} %sgt_hbm.1, ...), custom_call_target="tpu_custom_call" | custom-call | tf_op jit(solution)/shard_map/spectral_accelerations/pallas_call | solution.py:483
  61.5 1.3 %copy.11 = f32[1,4,88]{2,1,0:T(4,128)} copy(f32[1,4,88]{2,1,0:T(4,128)} %spectral_accelerations.1) | data formatting | bytes 2816

commit v5 on v4

--- a/solution.py
+++ b/solution.py
@@ -162,25 +162,6 @@
 
     loads[0].wait()
     weights_of(0)
-    for copy in copies:
-        copy.wait()
-    copies = []
-    for d, peer in enumerate(z_peers):
-        target = lax.rem(z + d + 1, NZ)
-        copy = remote(plane.at[:, target], block.at[y, z], send_b.at[d], recv_b.at[d], peer)
-        copy.start()
-        copies.append(copy)
-    block[y, z] = plane[:, z]
-    spread = []
-
-    def forward(turn, row):
-        for d, peer in enumerate(y_peers):
-            copy = remote(block.at[y, row], block.at[y, row], send_c.at[turn, d], recv_c.at[turn, d], peer)
-            copy.start()
-            spread.append(copy)
-
-    forward(0, z)
-
     for load in index_loads:
         load.wait()
 
@@ -200,6 +181,25 @@
         return carry
 
     lax.fori_loop(0, OWNERS, choose, 0)
+    for copy in copies:
+        copy.wait()
+    copies = []
+    for d, peer in enumerate(z_peers):
+        target = lax.rem(z + d + 1, NZ)
+        copy = remote(plane.at[:, target], block.at[y, z], send_b.at[d], recv_b.at[d], peer)
+        copy.start()
+        copies.append(copy)
+    block[y, z] = plane[:, z]
+    spread = []
+
+    def forward(turn, row):
+        for d, peer in enumerate(y_peers):
+            copy = remote(block.at[y, row], block.at[y, row], send_c.at[turn, d], recv_c.at[turn, d], peer)
+            copy.start()
+            spread.append(copy)
+
+    forward(0, z)
+
     for d, copy in enumerate(copies):
         copy.wait_recv()
         forward(d + 1, lax.rem(z + NZ - d - 1, NZ))
@@ -231,7 +231,7 @@
         fields_ref[2, pl.ds(row, 1), :] = block[at + (2,)]
         return carry
 
-    lax.fori_loop(0, OWNERS, select, 0)
+    lax.fori_loop(0, OWNERS, select, 0, unroll=8)
 
     amp = fields_ref[0]
     turns = fields_ref[1] * jnp.float32(TURNS)
@@ -299,7 +299,7 @@
         sources_of(turn, 1)
         return carry
 
-    pieces = [(0, 8), (8, 8), (16, 4), (20, 4), (24, 4), (28, 4)]
+    pieces = [(0, 8), (8, 8), (16, 4), (20, 4), (24, 4), (28, 2), (30, 2)]
 
     def send_parts(index):
         at, size = pieces[index]
@@ -349,7 +349,6 @@
         total = landed[0, h * 32 : h * 32 + 32]
         for src in range(1, NZ):
             total = total + landed[src, h * 32 : h * 32 + 32]
-        size = 8 if h < 2 else 4
         moved = [total] + [pltpu.roll(total, 32 * d, 1) for d in range(1, 4)]
         segment = lax.shift_right_logical(lane, 5)
 
@@ -357,7 +356,8 @@
             rows = []
             for g in range(4):
                 group = g * 2 + parity
-                row = group // size * 4 * size + slot * size + group % size
+                at, size = next(p for p in pieces if p[0] <= 8 * h + group < p[0] + p[1])
+                row = 4 * (at - 8 * h) + slot * size + 8 * h + group - at
                 rows.append(moved[(g - k) % 4][row : row + 1])
             return jnp.where(segment < 2, jnp.where(segment < 1, rows[0], rows[1]), jnp.where(segment < 3, rows[2], rows[3]))
 
@@ -423,7 +423,7 @@
             best[rows] = most
             return carry
 
-        lax.fori_loop(0, 4, tile, 0)
+        lax.fori_loop(0, 4, tile, 0, unroll=2)
 
     first_hop, second_hop = {}, {}
     inverse_load.wait()
@@ -445,19 +445,24 @@
     lax.fori_loop(13, 15, turn_of, 0)
     first_hop[4] = send_parts(4)
     second_hop[2] = send_sums(2, first_hop[2])
-    lax.fori_loop(15, 16, turn_of, 0)
+    sums_of(14, 1)
+    sources_of(15, 0)
+    first_hop[5] = send_parts(5)
+    sums_of(15, 0)
+    sources_of(15, 1)
     sums_of(15, 1)
-    first_hop[5] = send_parts(5)
+    first_hop[6] = send_parts(6)
     second_hop[3] = send_sums(3, first_hop[3])
     second_hop[4] = send_sums(4, first_hop[4])
     respond(1, second_hop[1])
     table_load.wait()
     add_series(0)
     second_hop[5] = send_sums(5, first_hop[5])
+    second_hop[6] = send_sums(6, first_hop[6])
     add_series(1)
     respond(2, second_hop[2] + second_hop[3])
     add_series(2)
-    respond(3, second_hop[4] + second_hop[5])
+    respond(3, second_hop[4] + second_hop[5] + second_hop[6])
     last_series(3)
 
     turned = [jnp.transpose(best[at : at + 128]) for at in range(0, ROWS, 128)]
@@ -517,7 +522,7 @@
             pltpu.VMEM((2, 2, ROWS, HALF), F32),
             pltpu.VMEM((ROWS, 128), F32),
             dma((10,)), dma((31,)), dma((31,)), dma((7,)), dma((7,)), dma((8, 3)), dma((8, 3)),
-            dma((6, 7)), dma((6, 7)), dma((6, 7)), dma((6, 7)),
+            dma((7, 7)), dma((7, 7)), dma((7, 7)), dma((7, 7)),
         ],
         compiler_params=pltpu.CompilerParams(
             collective_id=0, has_side_effects=True, vmem_limit_bytes=60 * 2**20

time: 62.8 us -> 61.7 us (0.982)
  Pallas kernels: 61.5 us -> 60.3 us
    pallas_call x1, Pallas kernels: 61.5 us -> 60.3 us  [program(): pl.pallas_call(kernel, out_shape=jax.ShapeDtypeStruct((1, 4, 2 * PERIODS)...]
where the time goes in v5:
time: 61.7 us; the launch traced here: 61.6 us
  Pallas kernels  60.3 us (98%)
  local copies, waits for them, and re-layouts  1.26 us (2%)
    pallas_call x1, Pallas kernels, program(): pl.pallas_call(kernel, out_shape=jax.ShapeDtypeStruct((1, 4, 2 * PERIODS)...  60.3 us
    unnamed x1, local copies, waits for them, and re-layouts  1.26 us

profile of v5, /device:TPU:1, one launch (start us, length us, event | category | flops | bytes accessed | tf_op | source)
XLA Modules:
  0.0 61.6 jit_solution(1164492446460067235)
XLA Ops:
  0.0 60.3 %spectral_accelerations.1 = f32[1,4,88]{2,1,0:T(4,128)} custom-call(s32[256]{0:T(256)} %start_hbm.1, s32[256]{0:T(256)} %count_hbm.1, s32[256]{0:T(256)} %order_hbm.1, f32[1024,8,128]{2,1,0:T(8,128)} %constant.6.clone.inverse_hbm, f32[3,4,2048]{2,1,0:T(4,128)} %bitcast.1, f32[6,128]{1,0:T(8,128)} %mech_hbm.1, bf16[1,2,6,2,128,1024]{5,4,3,2,1,0:T(8,128)(2,1)} %sgt_hbm.1, ...), custom_call_target="tpu_custom_call" | custom-call | tf_op jit(solution)/shard_map/spectral_accelerations/pallas_call | solution.py:488
  60.3 1.3 %copy.11 = f32[1,4,88]{2,1,0:T(4,128)} copy(f32[1,4,88]{2,1,0:T(4,128)} %spectral_accelerations.1) | data formatting | bytes 2816
